TPU v7x, 32 devices: a whole 2x2x4 slice. The times are simulated.
32 devices in a mesh: node: 4 (over z), local: 2 (over x), dp: 4 (over y, core).
Axes of the slice: x: 2, y: 2, z: 4, core: 2. Of those that a mesh axis runs over, the one named last changes fastest.
Arguments:
- layer_input: bfloat16 [2048, 2560], P(('node', 'dp'), 'local'), may hold values from -6 to 6
- grad_out: bfloat16 [2048, 2560], P(('node', 'dp'), 'local'), may hold values from -6 to 6
- gate_values: bfloat16 [2048, 6], P(('node', 'dp')), may hold values from 0.049804688 to 0.5
- route_expert: int32 [2048, 6], P(('node', 'dp')), may hold values from 0 to 39, as said below
- route_slot: int32 [2048, 6], P(('node', 'dp')), may hold values from -1 to 5, as said below
- shared_gate: bfloat16 [1536, 2560], P('local', 'dp'), may hold values from -0.125 to 0.125
- shared_up: bfloat16 [1536, 2560], P('local', 'dp'), may hold values from -0.125 to 0.125
- shared_down: bfloat16 [1536, 2560], P('local', 'dp'), may hold values from -0.15625 to 0.15625
- expert_gate: bfloat16 [16, 768, 2560], P(('node', 'dp'), 'local'), may hold values from -0.125 to 0.125
- expert_up: bfloat16 [16, 768, 2560], P(('node', 'dp'), 'local'), may hold values from -0.125 to 0.125
- expert_down: bfloat16 [16, 768, 2560], P(('node', 'dp'), 'local'), may hold values from -0.21875 to 0.21875
Outputs:
- grad_x: bfloat16 [2048, 2560], P(('node', 'dp'), 'local')
- grad_gates: float32 [2048, 6], P(('node', 'dp'))
- grad_shared_gate: bfloat16 [1536, 2560], P('local', 'dp')
- grad_shared_up: bfloat16 [1536, 2560], P('local', 'dp')
- grad_shared_down: bfloat16 [1536, 2560], P('local', 'dp')
- grad_expert_gate: bfloat16 [16, 768, 2560], P(('node', 'dp'), 'local')
- grad_expert_up: bfloat16 [16, 768, 2560], P(('node', 'dp'), 'local')
- grad_expert_down: bfloat16 [16, 768, 2560], P(('node', 'dp'), 'local')
Inputs may be any that keep to these rules, and one draw needn't show every extreme that they name: `route_expert`: each row names 6 different experts, all on at most 3 nodes; expert i lies on node i // 10. `route_slot`: for the choice of expert i, counting the choices of the 128 tokens of one group to the same expert in the order of rows, then of columns, from 0: the slot is that count, and it is -1 exactly where i % 10 >= 4 or the count reaches 6.
All inputs are finite; a program needn't handle non-finite values.
Results may differ from a plain program's by a relative error of at most 0.025.
Values may be sent and summed in bfloat16 or wider, within the bound.
No kernel may reach another device: no remote copies, remote signals or barrier semaphores. Data moves between devices by JAX's collectives and lax.ppermute only.
A program may use at most 128 MiB of HBM per device.

v0:
```python
import jax
import jax.numpy as jnp
from jax import lax
from jax.sharding import PartitionSpec as P

NODE_EXPERTS = 10
CAP = 6


def contract_rows(left, right):
    return lax.dot_general(
        left, right, (((0,), (0,)), ((), ())), preferred_element_type=jnp.float32
    )


def contract_cols(left, right):
    return lax.dot_general(
        left, right, (((1,), (1,)), ((), ())), preferred_element_type=jnp.float32
    )


def on_device(
    layer_input,
    grad_out,
    gate_values,
    route_expert,
    route_slot,
    shared_gate,
    shared_up,
    shared_down,
    expert_gate,
    expert_up,
    expert_down,
):
    n_node = lax.axis_size("node")
    n_dp = lax.axis_size("dp")
    groups = n_node * n_dp
    feat_slice = layer_input.shape[1]
    slot_count = groups * CAP
    full_x, full_dy = (
        lax.all_gather(layer_input, "local", axis=1, tiled=True),
        lax.all_gather(grad_out, "local", axis=1, tiled=True),
    )
    kept = route_slot >= 0
    held = route_expert // NODE_EXPERTS * n_dp + route_expert % NODE_EXPERTS
    position = jnp.where(kept, held * CAP + route_slot, -1)
    slot_ids = jnp.arange(slot_count, dtype=jnp.int32)
    matches = position[None, :, :] == slot_ids[:, None, None]
    select = jnp.any(matches, axis=2).astype(jnp.bfloat16)
    slot_gate = jnp.sum(
        jnp.where(matches, gate_values.astype(jnp.float32)[None, :, :], 0.0), axis=(1, 2)
    ).astype(jnp.bfloat16)
    send_x = jnp.dot(select, full_x, preferred_element_type=jnp.float32).astype(jnp.bfloat16)
    send_dy = jnp.dot(select, full_dy, preferred_element_type=jnp.float32).astype(jnp.bfloat16)
    row_width = send_x.shape[1]
    recv_x, recv_dy, recv_gate = (
        lax.all_to_all(
            send_x.reshape(groups, CAP, row_width),
            ("node", "dp"),
            split_axis=0,
            concat_axis=0,
            tiled=True,
        ),
        lax.all_to_all(
            send_dy.reshape(groups, CAP, row_width),
            ("node", "dp"),
            split_axis=0,
            concat_axis=0,
            tiled=True,
        ),
        lax.all_to_all(
            slot_gate.reshape(groups, CAP), ("node", "dp"), split_axis=0, concat_axis=0, tiled=True
        ),
    )
    model_width = recv_x.shape[2]
    rows_x = recv_x.reshape(slot_count, model_width)
    rows_dy = recv_dy.reshape(slot_count, model_width)
    weight_q = recv_gate.reshape(slot_count).astype(jnp.float32)[:, None]
    weight_gate = expert_gate[0]
    weight_up = expert_up[0]
    weight_down = expert_down[0]
    feature_gate, feature_up = (
        lax.all_to_all(weight_gate, "local", split_axis=1, concat_axis=0, tiled=True),
        lax.all_to_all(weight_up, "local", split_axis=1, concat_axis=0, tiled=True),
    )
    pre_a = contract_cols(rows_x, weight_gate)
    pre_b = contract_cols(rows_x, weight_up)
    back_e = contract_cols(rows_dy, weight_down)
    sigm_a = jax.nn.sigmoid(pre_a)
    silu_a = pre_a * sigm_a
    hidden = silu_a * pre_b
    gate_part = jnp.sum(back_e * hidden, axis=1).reshape(groups, CAP)
    gate_grad = lax.psum(gate_part, "local")
    grad_a = (weight_q * back_e * pre_b * sigm_a * (1.0 + pre_a * (1.0 - sigm_a))).astype(
        jnp.bfloat16
    )
    grad_b = (weight_q * back_e * silu_a).astype(jnp.bfloat16)
    hidden_q = (weight_q * hidden).astype(jnp.bfloat16)
    new_gate = contract_rows(grad_a, rows_x).astype(jnp.bfloat16)
    new_up = contract_rows(grad_b, rows_x).astype(jnp.bfloat16)
    new_down = contract_rows(hidden_q, rows_dy).astype(jnp.bfloat16)
    total = jnp.dot(
        lax.all_gather(grad_a, "local", axis=1, tiled=True),
        feature_gate,
        preferred_element_type=jnp.float32,
    )
    row_dx = total + jnp.dot(
        lax.all_gather(grad_b, "local", axis=1, tiled=True),
        feature_up,
        preferred_element_type=jnp.float32,
    )
    back_dx, back_gate = (
        lax.all_to_all(
            row_dx.reshape(groups, CAP, feat_slice).astype(jnp.bfloat16),
            ("node", "dp"),
            split_axis=0,
            concat_axis=0,
            tiled=True,
        ).astype(jnp.float32),
        lax.all_to_all(
            gate_grad.astype(jnp.bfloat16), ("node", "dp"), split_axis=0, concat_axis=0, tiled=True
        ).astype(gate_grad.dtype),
    )
    back_rows = back_dx.reshape(slot_count, feat_slice)
    routed_dx = lax.dot_general(
        select.astype(jnp.float32),
        back_rows,
        (((0,), (0,)), ((), ())),
        precision=lax.Precision.HIGHEST,
        preferred_element_type=jnp.float32,
    )
    back_flat = back_gate.reshape(slot_count)
    grad_gates = jnp.sum(jnp.where(matches, back_flat[:, None, None], 0.0), axis=0)
    share_gate, share_up, share_down = (
        lax.all_gather(shared_gate, "dp", axis=1, tiled=True),
        lax.all_gather(shared_up, "dp", axis=1, tiled=True),
        lax.all_gather(shared_down, "dp", axis=1, tiled=True),
    )
    shared_a = contract_cols(full_x, share_gate)
    shared_b = contract_cols(full_x, share_up)
    shared_e = contract_cols(full_dy, share_down)
    sigm_s = jax.nn.sigmoid(shared_a)
    silu_s = shared_a * sigm_s
    shared_h = (silu_s * shared_b).astype(jnp.bfloat16)
    shared_da = (shared_e * shared_b * sigm_s * (1.0 + shared_a * (1.0 - sigm_s))).astype(
        jnp.bfloat16
    )
    shared_db = (shared_e * silu_s).astype(jnp.bfloat16)
    dx_part = jnp.dot(shared_da, share_gate, preferred_element_type=jnp.float32)
    dx_part = dx_part + jnp.dot(shared_db, share_up, preferred_element_type=jnp.float32)
    shared_dx = lax.psum_scatter(
        dx_part.astype(jnp.bfloat16), "local", scatter_dimension=1, tiled=True
    ).astype(jnp.float32)
    part_gate = contract_rows(shared_da, full_x)
    part_up = contract_rows(shared_db, full_x)
    part_down = contract_rows(shared_h, full_dy)
    sum_gate, sum_up, sum_down = (
        lax.psum_scatter(
            part_gate.astype(jnp.bfloat16), "dp", scatter_dimension=1, tiled=True
        ).astype(jnp.float32),
        lax.psum_scatter(
            part_up.astype(jnp.bfloat16), "dp", scatter_dimension=1, tiled=True
        ).astype(jnp.float32),
        lax.psum_scatter(
            part_down.astype(jnp.bfloat16), "dp", scatter_dimension=1, tiled=True
        ).astype(jnp.float32),
    )
    sum_gate, sum_up, sum_down = (
        lax.psum(sum_gate.astype(jnp.bfloat16), "node").astype(jnp.float32),
        lax.psum(sum_up.astype(jnp.bfloat16), "node").astype(jnp.float32),
        lax.psum(sum_down.astype(jnp.bfloat16), "node").astype(jnp.float32),
    )
    grad_x = (shared_dx + routed_dx).astype(jnp.bfloat16)
    return (
        grad_x,
        grad_gates,
        sum_gate.astype(jnp.bfloat16),
        sum_up.astype(jnp.bfloat16),
        sum_down.astype(jnp.bfloat16),
        new_gate[None],
        new_up[None],
        new_down[None],
    )


def solution(mesh):
    in_specs = (
        P(("node", "dp"), "local"),
        P(("node", "dp"), "local"),
        P(("node", "dp"), None),
        P(("node", "dp"), None),
        P(("node", "dp"), None),
        P("local", "dp"),
        P("local", "dp"),
        P("local", "dp"),
        P(("node", "dp"), "local", None),
        P(("node", "dp"), "local", None),
        P(("node", "dp"), "local", None),
    )
    out_specs = (
        P(("node", "dp"), "local"),
        P(("node", "dp"), None),
        P("local", "dp"),
        P("local", "dp"),
        P("local", "dp"),
        P(("node", "dp"), "local", None),
        P(("node", "dp"), "local", None),
        P(("node", "dp"), "local", None),
    )
    return jax.shard_map(
        on_device, mesh=mesh, in_specs=in_specs, out_specs=out_specs, check_vma=False
    )
```

profile of v0, /device:TPU:0, one launch (start us, length us, event | category | flops | bytes accessed | tf_op | source)
XLA Modules:
  0.0 428.8 jit_solution(2209447473407653824)
XLA Ops:
  9.5 11.3 %all_gather.23 = bf16[128,2560]{1,0:T(8,128)(2,1)S(1)} all-gather(bf16[128,1280]{1,0:T(8,128)(2,1)S(1)} %copy-done.13), channel_id=1, replica_groups=mesh['node'=4,'local'=2,'dp'=4] {'local'}, dimensions={1}, use_global_device_ids=true | all-gather | bytes 983040 | tf_op jit(solution)/shard_map/all_gather | solution.py:41
  20.8 9.8 %all_gather.21 = bf16[128,2560]{1,0:T(8,128)(2,1)S(1)} all-gather(bf16[128,1280]{1,0:T(8,128)(2,1)} %param.12), channel_id=1, replica_groups=mesh['node'=4,'local'=2,'dp'=4] {'local'}, dimensions={1}, use_global_device_ids=true | all-gather | bytes 983040 | tf_op jit(solution)/shard_map/all_gather | solution.py:42
  30.6 14.7 %all-gather.8.cloned.1.call-done = bf16[768,2560]{1,0:T(8,128)(2,1)} async-done(((bf16[768,640]{1,0:T(8,128)(2,1)}), bf16[768,2560]{1,0:T(8,128)(2,1)}) %all-gather.8.cloned.1.call-update) | async-done | bytes 3932176 | tf_op jit(solution)/shard_map/all_gather | solution.py:135
  49.5 30.4 %all-gather.6.cloned.1.call-done = bf16[768,2560]{1,0:T(8,128)(2,1)} async-done(((bf16[768,640]{1,0:T(8,128)(2,1)}), bf16[768,2560]{1,0:T(8,128)(2,1)}) %all-gather.6.cloned.1.call-update) | async-done | bytes 3932176 | tf_op jit(solution)/shard_map/all_gather | solution.py:136
  84.1 30.4 %all-gather.4.cloned.1.call-done = bf16[768,2560]{1,0:T(8,128)(2,1)} async-done(((bf16[768,640]{1,0:T(8,128)(2,1)}), bf16[768,2560]{1,0:T(8,128)(2,1)}) %all-gather.4.cloned.1.call-update) | async-done | bytes 3932176 | tf_op jit(solution)/shard_map/all_gather | solution.py:137
  122.0 6.2 %copy.58 = bf16[768,2560]{0,1:T(8,128)(2,1)} copy(bf16[768,2560]{1,0:T(8,128)(2,1)} %convolution_convert_fusion.2) | data formatting | bytes 7864320
  131.3 6.4 %copy.60 = bf16[768,2560]{0,1:T(8,128)(2,1)} copy(bf16[768,2560]{1,0:T(8,128)(2,1)} %convolution_convert_fusion.1) | data formatting | bytes 7864320
  137.8 4.3 %convolution_convert_fusion = bf16[768,2560]{1,0:T(8,128)(2,1)} fusion(bf16[128,2560]{1,0:T(8,128)(2,1)S(1)} %all_gather.21, f32[128,768]{1,0:T(8,128)} %fusion.26, f32[128,768]{1,0:T(8,128)} %fusion.27), kind=kOutput, calls=%fused_computation | convolution fusion | flops 505872384 | bytes 5373952 | tf_op jit(solution)/shard_map/dot_general | solution.py:11
  142.1 6.3 %copy.62 = bf16[768,2560]{0,1:T(8,128)(2,1)} copy(bf16[768,2560]{1,0:T(8,128)(2,1)} %convolution_convert_fusion) | data formatting | bytes 7864320
  152.3 4.7 %all-to-all-start.2 = ((bf16[16,6,2560]{2,1,0:T(8,128)(2,1)}), bf16[16,6,2560]{2,1,0:T(8,128)(2,1)S(1)}, u32[]{:S(2)}, u32[]{:S(2)}) async-start(bf16[16,6,2560]{2,1,0:T(8,128)(2,1)} %reshape.81), calls=%async_computation.3 | async-start | bytes 1310720 | tf_op jit(solution)/shard_map/all_to_all | solution.py:57
  160.1 13.5 %all-to-all-done.2 = bf16[16,6,2560]{2,1,0:T(8,128)(2,1)S(1)} async-done(((bf16[16,6,2560]{2,1,0:T(8,128)(2,1)}), bf16[16,6,2560]{2,1,0:T(8,128)(2,1)S(1)}, u32[]{:S(2)}, u32[]{:S(2)}) %all-to-all-start.2) | async-done | bytes 491552 | tf_op jit(solution)/shard_map/all_to_all | solution.py:57
  173.6 4.8 %all-to-all-start.1 = ((bf16[16,6,2560]{2,1,0:T(8,128)(2,1)}), bf16[16,6,2560]{2,1,0:T(8,128)(2,1)}, u32[]{:S(2)}, u32[]{:S(2)}) async-start(bf16[16,6,2560]{2,1,0:T(8,128)(2,1)} %reshape.79), calls=%async_computation.2 | async-start | bytes 1310720 | tf_op jit(solution)/shard_map/all_to_all | solution.py:64
  179.8 15.3 %all-to-all-done.1 = bf16[16,6,2560]{2,1,0:T(8,128)(2,1)} async-done(((bf16[16,6,2560]{2,1,0:T(8,128)(2,1)}), bf16[16,6,2560]{2,1,0:T(8,128)(2,1)}, u32[]{:S(2)}, u32[]{:S(2)}) %all-to-all-start.1) | async-done | bytes 491552 | tf_op jit(solution)/shard_map/all_to_all | solution.py:64
  205.9 4.9 %psum.28 = bf16[16,6]{0,1:T(8,128)(2,1)S(1)} all-reduce(f32[16,6]{0,1:T(8,128)S(1)} %copy.56), channel_id=1, replica_groups=mesh['node'=4,'local'=2,'dp'=4] {'local'}, use_global_device_ids=true, to_apply=%region_4.5 | all-reduce | flops 96 | bytes 576 | tf_op jit(solution)/shard_map/psum | solution.py:93
  211.5 4.4 %all-to-all-start.6 = ((bf16[16,1,6]{2,1,0:T(2,128)(2,1)}), bf16[16,1,6]{2,1,0:T(2,128)(2,1)S(1)}, u32[]{:S(2)}, u32[]{:S(2)}) async-start(bf16[16,1,6]{2,1,0:T(2,128)(2,1)} %copy.57), calls=%async_computation.7 | async-start | bytes 16384 | tf_op jit(solution)/shard_map/all_to_all | solution.py:120
  216.0 6.3 %all-to-all-done.6 = bf16[16,1,6]{2,1,0:T(2,128)(2,1)S(1)} async-done(((bf16[16,1,6]{2,1,0:T(2,128)(2,1)}), bf16[16,1,6]{2,1,0:T(2,128)(2,1)S(1)}, u32[]{:S(2)}, u32[]{:S(2)}) %all-to-all-start.6) | async-done | bytes 224 | tf_op jit(solution)/shard_map/all_to_all | solution.py:120
  233.6 4.8 %all-to-all-start.3 = ((bf16[384,2,1280]{0,2,1:T(8,128)(2,1)}), bf16[384,2,1280]{0,2,1:T(8,128)(2,1)}, u32[]{:S(2)}, u32[]{:S(2)}) async-start(bf16[384,2,1280]{0,2,1:T(8,128)(2,1)} %bitcast.68), calls=%async_computation.4 | async-start | bytes 3932160 | tf_op jit(solution)/shard_map/all_to_all | solution.py:83
  243.2 25.9 %reduce-scatter.17.cloned.1.call-done = bf16[640,768]{1,0:T(8,128)(2,1)} async-done(((bf16[2560,768]{1,0:T(8,128)(2,1)}), bf16[640,768]{1,0:T(8,128)(2,1)}) %reduce-scatter.17.cloned.1.call-update) | async-done | bytes 983056
  275.3 4.8 %all-to-all-start.4 = ((bf16[384,2,1280]{0,2,1:T(8,128)(2,1)}), bf16[384,2,1280]{0,2,1:T(8,128)(2,1)}, u32[]{:S(2)}, u32[]{:S(2)}) async-start(bf16[384,2,1280]{0,2,1:T(8,128)(2,1)} %bitcast.69), calls=%async_computation.5 | async-start | bytes 3932160 | tf_op jit(solution)/shard_map/all_to_all | solution.py:84
  280.3 28.8 %all_gather.26 = bf16[96,768]{1,0:T(8,128)(2,1)S(1)} all-gather(bf16[96,384]{1,0:T(8,128)(2,1)S(1)} %get-tuple-element.16), channel_id=1, replica_groups=mesh['node'=4,'local'=2,'dp'=4] {'local'}, dimensions={1}, use_global_device_ids=true | all-gather | bytes 221184 | tf_op jit(solution)/shard_map/all_gather | solution.py:103
  309.1 5.1 %all_gather.27 = bf16[96,768]{1,0:T(8,128)(2,1)} all-gather(bf16[96,384]{1,0:T(8,128)(2,1)S(1)} %get-tuple-element.15), channel_id=1, replica_groups=mesh['node'=4,'local'=2,'dp'=4] {'local'}, dimensions={1}, use_global_device_ids=true | all-gather | bytes 221184 | tf_op jit(solution)/shard_map/all_gather | solution.py:108
  325.6 5.8 %all-to-all-start.5 = ((bf16[16,6,1280]{2,1,0:T(8,128)(2,1)}), bf16[16,6,1280]{2,1,0:T(8,128)(2,1)}, u32[]{:S(2)}, u32[]{:S(2)}) async-start(bf16[16,6,1280]{2,1,0:T(8,128)(2,1)} %convert_element_type.126), calls=%async_computation.6 | async-start | bytes 655360 | tf_op jit(solution)/shard_map/all_to_all | solution.py:113
  338.3 10.0 %all-to-all-done.5 = bf16[16,6,1280]{2,1,0:T(8,128)(2,1)} async-done(((bf16[16,6,1280]{2,1,0:T(8,128)(2,1)}), bf16[16,6,1280]{2,1,0:T(8,128)(2,1)}, u32[]{:S(2)}, u32[]{:S(2)}) %all-to-all-start.5) | async-done | bytes 245792 | tf_op jit(solution)/shard_map/all_to_all | solution.py:113
  351.3 66.3 %all-reduce.3.cloned.1.call-done = (bf16[768,640]{1,0:T(8,128)(2,1)}, bf16[768,640]{1,0:T(8,128)(2,1)}, bf16[768,640]{1,0:T(8,128)(2,1)}) async-done(((bf16[768,640]{1,0:T(8,128)(2,1)}, bf16[768,640]{1,0:T(8,128)(2,1)}, bf16[768,640]{1,0:T(8,128)(2,1)}), (bf16[768,640]{1,0:T(8,128)(2,1)}, bf16[768,640]{1,0:T(8,128)(2,1)}, bf16[768,640]{1,0:T(8,128)(2,1)})) %all-reduce.3.cloned.1.call-update) | async-done | bytes 2949136 | tf_op jit(solution)/shard_map/psum | solution.py:169
  (104 shorter events, 89.0 us)
Async XLA Ops:
  7.2 197.7 %copy-start = (bf16[1,384,2560]{2,1,0:T(8,128)(2,1)S(1)}, bf16[1,384,2560]{2,1,0:T(8,128)(2,1)}, u32[]{:S(2)}) copy-start(bf16[1,384,2560]{2,1,0:T(8,128)(2,1)} %param.21) | copy-start | bytes 5898244
  7.2 38.1 %all-gather.8.cloned.1.call-start = ((), (), s32[]{:S(2)}) async-start(), calls=%async_computation.13 | async-start | bytes 4915200 | tf_op jit(solution)/shard_map/all_gather | solution.py:135
  7.9 71.9 %all-gather.6.cloned.1.call-start = ((), (), s32[]{:S(2)}) async-start(), calls=%async_computation.12 | async-start | bytes 4915200 | tf_op jit(solution)/shard_map/all_gather | solution.py:136
  8.7 105.8 %all-gather.4.cloned.1.call-start = ((), (), s32[]{:S(2)}) async-start(), calls=%async_computation.11 | async-start | bytes 4915200 | tf_op jit(solution)/shard_map/all_gather | solution.py:137
  9.4 229.3 %reduce-scatter.13.cloned.1.call-start = ((), (), s32[]{:S(2)}) async-start(), calls=%async_computation.15 | async-start | bytes 4915200
  128.2 112.8 %reduce-scatter.15.cloned.1.call-start = ((), (), s32[]{:S(2)}) async-start(), calls=%async_computation.16 | async-start | bytes 4915200
  137.7 131.3 %reduce-scatter.17.cloned.1.call-start = ((), (), s32[]{:S(2)}) async-start(), calls=%async_computation.17 | async-start | bytes 4915200
  152.3 21.3 %all-to-all-start.2 = ((bf16[16,6,2560]{2,1,0:T(8,128)(2,1)}), bf16[16,6,2560]{2,1,0:T(8,128)(2,1)S(1)}, u32[]{:S(2)}, u32[]{:S(2)}) async-start(bf16[16,6,2560]{2,1,0:T(8,128)(2,1)} %reshape.81), calls=%async_computation.3 | async-start | bytes 1310720 | tf_op jit(solution)/shard_map/all_to_all | solution.py:57
  160.1 36.3 %copy-start.6 = (bf16[128,768]{1,0:T(8,128)(2,1)S(1)}, bf16[128,768]{1,0:T(8,128)(2,1)}, u32[]{:S(2)}) copy-start(bf16[128,768]{1,0:T(8,128)(2,1)} %copy-done.5) | copy-start | bytes 589828
  173.6 4.8 %copy-start.4 = (bf16[16,6,2560]{2,1,0:T(8,128)(2,1)}, bf16[16,6,2560]{2,1,0:T(8,128)(2,1)S(1)}, u32[]{:S(2)}) copy-start(bf16[16,6,2560]{2,1,0:T(8,128)(2,1)S(1)} %all-to-all-done.2) | copy-start | bytes 1474564
  173.6 21.5 %all-to-all-start.1 = ((bf16[16,6,2560]{2,1,0:T(8,128)(2,1)}), bf16[16,6,2560]{2,1,0:T(8,128)(2,1)}, u32[]{:S(2)}, u32[]{:S(2)}) async-start(bf16[16,6,2560]{2,1,0:T(8,128)(2,1)} %reshape.79), calls=%async_computation.2 | async-start | bytes 1310720 | tf_op jit(solution)/shard_map/all_to_all | solution.py:64
  178.5 170.9 %reduce-scatter.11.cloned.1.call-start = ((), (), s32[]{:S(2)}) async-start(), calls=%async_computation.14 | async-start | bytes 983040 | tf_op jit(solution)/shard_map/reduce_scatter | solution.py:151
  196.4 3.8 copy-start.1
  204.9 11.1 %copy-start.16 = (bf16[128,6]{0,1:T(8,128)(2,1)S(1)}, bf16[128,6]{0,1:T(8,128)(2,1)}, u32[]{:S(2)}) copy-start(bf16[128,6]{0,1:T(8,128)(2,1)} %param.13) | copy-start | bytes 4612
  211.5 10.7 %all-to-all-start.6 = ((bf16[16,1,6]{2,1,0:T(2,128)(2,1)}), bf16[16,1,6]{2,1,0:T(2,128)(2,1)S(1)}, u32[]{:S(2)}, u32[]{:S(2)}) async-start(bf16[16,1,6]{2,1,0:T(2,128)(2,1)} %copy.57), calls=%async_computation.7 | async-start | bytes 16384 | tf_op jit(solution)/shard_map/all_to_all | solution.py:120
  223.8 9.8 %all-to-all-start = ((bf16[16,1,6]{2,1,0:T(2,128)(2,1)}), bf16[16,1,6]{2,1,0:T(2,128)(2,1)S(1)}, u32[]{:S(2)}, u32[]{:S(2)}) async-start(bf16[16,1,6]{2,1,0:T(2,128)(2,1)} %convert_element_type.141), calls=%async_computation.1 | async-start | bytes 16384 | tf_op jit(solution)/shard_map/all_to_all | solution.py:71
  233.6 41.7 %all-to-all-start.3 = ((bf16[384,2,1280]{0,2,1:T(8,128)(2,1)}), bf16[384,2,1280]{0,2,1:T(8,128)(2,1)}, u32[]{:S(2)}, u32[]{:S(2)}) async-start(bf16[384,2,1280]{0,2,1:T(8,128)(2,1)} %bitcast.68), calls=%async_computation.4 | async-start | bytes 3932160 | tf_op jit(solution)/shard_map/all_to_all | solution.py:83
  238.4 179.3 %all-reduce.3.cloned.1.call-start = ((), (), s32[]{:S(2)}) async-start(), calls=%async_computation.18 | async-start | bytes 5898240 | tf_op jit(solution)/shard_map/psum | solution.py:169
  275.3 42.9 %all-to-all-start.4 = ((bf16[384,2,1280]{0,2,1:T(8,128)(2,1)}), bf16[384,2,1280]{0,2,1:T(8,128)(2,1)}, u32[]{:S(2)}, u32[]{:S(2)}) async-start(bf16[384,2,1280]{0,2,1:T(8,128)(2,1)} %bitcast.69), calls=%async_computation.5 | async-start | bytes 3932160 | tf_op jit(solution)/shard_map/all_to_all | solution.py:84
  280.3 28.8 %copy-start.9 = (bf16[96,384]{1,0:T(8,128)(2,1)}, bf16[96,384]{1,0:T(8,128)(2,1)S(1)}, u32[]{:S(2)}) copy-start(bf16[96,384]{1,0:T(8,128)(2,1)S(1)} %get-tuple-element.15) | copy-start | bytes 221188
  280.3 33.9 %copy-start.11 = (bf16[96,384]{1,0:T(8,128)(2,1)}, bf16[96,384]{1,0:T(8,128)(2,1)S(1)}, u32[]{:S(2)}) copy-start(bf16[96,384]{1,0:T(8,128)(2,1)S(1)} %get-tuple-element.16) | copy-start | bytes 221188
  325.6 8.7 %copy-start.10 = (bf16[96,384]{1,0:T(8,128)(2,1)S(1)}, bf16[96,384]{1,0:T(8,128)(2,1)}, u32[]{:S(2)}) copy-start(bf16[96,384]{1,0:T(8,128)(2,1)} %copy-done.9) | copy-start | bytes 221188
  325.6 22.6 %all-to-all-start.5 = ((bf16[16,6,1280]{2,1,0:T(8,128)(2,1)}), bf16[16,6,1280]{2,1,0:T(8,128)(2,1)}, u32[]{:S(2)}, u32[]{:S(2)}) async-start(bf16[16,6,1280]{2,1,0:T(8,128)(2,1)} %convert_element_type.126), calls=%async_computation.6 | async-start | bytes 655360 | tf_op jit(solution)/shard_map/all_to_all | solution.py:113
  417.7 3.3 copy-start.7
  (8 other events, 13.5 us)
Sparse Core Ops, SparseCore 0:
  9.6 35.6 all-gather.7
  46.9 32.9 all-gather.5
  81.4 32.9 all-gather.3
  128.3 49.8 reduce-scatter.12
  180.8 42.9 reduce-scatter.14
  226.2 42.8 reduce-scatter.16
  271.4 19.5 reduce-scatter.10
  294.1 123.5 all-reduce.2
where the time goes:
time: 431 us; the launch traced here: 429 us
  waiting for transfers between devices  217 us (50%)
  blocking collectives  59.9 us (14%)
  local copies, waits for them, and re-layouts  58.1 us (13%)
  matrix products  44.7 us (10%)
  starting transfers between devices  33.2 us (8%)
  between operations  14.5 us (3%)
    psum x1, waiting for transfers between devices, on_device(): lax.psum(sum_gate.astype(jnp.bfloat16), 'node').astype(jnp.float32)  66.3 us
    unnamed x45, local copies, waits for them, and re-layouts  40 us
    all_gather x1, waiting for transfers between devices, on_device(): lax.all_gather(shared_down, 'dp', axis=1, tiled=True)  30.4 us
    all_gather x1, waiting for transfers between devices, on_device(): lax.all_gather(shared_up, 'dp', axis=1, tiled=True)  30.4 us
    all_gather x1, blocking collectives, on_device(): lax.all_gather(grad_a, 'local', axis=1, tiled=True)  28.8 us
    unnamed x11, waiting for transfers between devices  28.1 us
    dot_general x6, matrix products, contract_rows(): lax.dot_general(left, right, (((0,), (0,)), ((), ())), preferred_element_...  17.4 us
    dot_general x6, matrix products, contract_cols(): lax.dot_general(left, right, (((1,), (1,)), ((), ())), preferred_element_...  16.1 us
  transfers between devices with their start and end apart: 15, of which 10 were waited for; matrix products, arithmetic and copies ran while one was open for 20% of the time, Pallas kernels for 0%

commit v1 on v0

v1 whole, which is shorter than its diff:
```python
import functools

import jax
import jax.numpy as jnp
from jax import lax
from jax.experimental import pallas as pl
from jax.experimental.pallas import tpu as pltpu
from jax.sharding import PartitionSpec as P

NODE_EXPERTS = 10
BLOCK = 8
GATE_ROW = 6
CORE, ALIGNED, LOCAL, MIDDLE = range(4)
VMEM_BYTES = 24 * 1024 * 1024
LINE_BYTES = 8 * 1024 * 1024
BF = jnp.bfloat16
F32 = jnp.float32

SMEM = pl.BlockSpec(memory_space=pltpu.SMEM)
VMEM = pl.BlockSpec(memory_space=pltpu.VMEM)
ANY = pl.BlockSpec(memory_space=pl.ANY)


def dot_rows(left, right):
    return lax.dot_general(left, right, (((0,), (0,)), ((), ())), preferred_element_type=F32)


def dot_cols(left, right):
    return lax.dot_general(left, right, (((1,), (1,)), ((), ())), preferred_element_type=F32)


def dot(left, right):
    return lax.dot_general(left, right, (((1,), (0,)), ((), ())), preferred_element_type=F32)


def whole(dims):
    zeros = (0,) * len(dims)
    return pl.BlockSpec(dims, lambda i: zeros)


def far(value):
    return ("far", pltpu.with_memory_space_constraint(value, pltpu.HBM))


def call(kernel, outs, operands, name, flags=(), after=(), held=(), vmem=VMEM_BYTES, far_outs=()):
    count = len(flags) + len(operands)
    first = count + len(after)

    def body(*refs):
        kernel(*refs[:count], *refs[first + len(held) : len(refs) - len(held)])

    specs = [whole(v[1].shape) if isinstance(v, tuple) else VMEM for v in operands]
    operands = [v[1] if isinstance(v, tuple) else v for v in operands]
    got = pl.pallas_call(
        body,
        grid=(1,),
        out_shape=[pltpu.HBM(v.shape, v.dtype) if i in far_outs else v for i, v in enumerate(outs)]
        + [shape(v.shape, v.dtype) for v in held],
        in_specs=[SMEM] * len(flags) + specs + [ANY] * (len(after) + len(held)),
        out_specs=[whole(v.shape) if i in far_outs else VMEM for i, v in enumerate(outs)]
        + [ANY] * len(held),
        input_output_aliases={first + i: len(outs) + i for i in range(len(held))},
        compiler_params=pltpu.CompilerParams(vmem_limit_bytes=vmem),
        cost_estimate=pl.CostEstimate(flops=0, bytes_accessed=0, transcendentals=0),
        name=name,
    )(*flags, *operands, *after, *held)
    return list(got)


def shape(dims, dtype):
    return jax.ShapeDtypeStruct(dims, dtype)


def positions(expert, slot, n_dp):
    node = (expert * 205) >> 11
    held = node * n_dp + expert - node * NODE_EXPERTS
    return jnp.where(slot >= 0, held * BLOCK + slot, -1)


def pack_kernel(*refs):
    rows = refs[0].shape[0]
    for index, ref in enumerate(refs[:-1]):
        refs[-1][index * rows : (index + 1) * rows] = ref[...]


def select_kernel(n_dp, expert_ref, slot_ref, gate_ref, x_ref, dy_ref, out_ref):
    choices, tokens = slot_ref.shape
    slots = out_ref.shape[0]
    width = x_ref.shape[1]
    line = lax.broadcasted_iota(jnp.int32, (slots, tokens), 0)
    pos = positions(expert_ref[...], slot_ref[...], n_dp)
    gate = gate_ref[...].astype(F32)
    sel = jnp.zeros((slots, tokens), F32)
    selq = jnp.zeros((slots, tokens), F32)
    for k in range(choices):
        hit = pos[k : k + 1] == line
        sel = jnp.where(hit, 1.0, sel)
        selq = jnp.where(hit, gate[k : k + 1], selq)
    out_ref[:, :width] = dot(sel.astype(BF), x_ref[...]).astype(BF)
    out_ref[:, width:] = dot(selq.astype(BF), dy_ref[...]).astype(BF)


def product_kernel(inputs, blocks, first, mats, flag_ref, *refs):
    source = refs[:inputs]
    own_ref, oth_ref, keep_ref, send_ref, mine_ref, *away = refs[inputs:]
    tokens, width = source[0].shape[0], keep_ref.shape[1]
    hidden = mine_ref.shape[1]
    core = flag_ref[CORE]
    for place, out in ((core, keep_ref), (1 - core, send_ref)):
        at = pl.ds(pl.multiple_of(place * width, 128), width)
        parts = [ref[:, at] for ref in source]
        if inputs > blocks:
            aligned = flag_ref[ALIGNED] == 1
            parts = [jnp.where(aligned, parts[0], parts[1]), jnp.where(aligned, parts[1], parts[2])]
        for j, part in enumerate(parts):
            out[j * tokens : (j + 1) * tokens] = part
    keep, send = keep_ref[...], send_ref[...]
    for index in range(mats):
        weight = slice((first + index) * hidden, (first + index + 1) * hidden)
        product = dot_cols(keep, own_ref[weight]) + dot_cols(send, oth_ref[weight])
        at = slice(index * tokens, (index + 1) * tokens)
        mine_ref[at] = product[:tokens]
        for j, ref in enumerate(away):
            ref[at] = product[(j + 1) * tokens : (j + 2) * tokens].astype(BF)


def slope_kernel(terms, *refs):
    def total(part):
        value = part[0][...]
        for ref in part[1:]:
            value = value + ref[...].astype(F32)
        return value

    both, e = total(refs[:terms]), total(refs[terms : 2 * terms])
    tokens = e.shape[0]
    a, b = both[:tokens], both[tokens:]
    sigm = jax.nn.sigmoid(a)
    silu = a * sigm
    values = (silu * b, e * b * sigm * (1.0 + a * (1.0 - sigm)), e * silu)
    for index, out in enumerate(refs[2 * terms :]):
        part = out.shape[1]
        for row, value in enumerate(values):
            out[row * tokens : (row + 1) * tokens] = value[:, index * part : (index + 1) * part].astype(BF)


def weight_grad_kernel(pieces, x_keep, x_recv, dy_keep, dy_recv, *refs):
    tokens = refs[0].shape[0] // 3
    x = jnp.concatenate([x_keep[...], x_recv[...]], axis=0)
    dy = jnp.concatenate([dy_keep[...], dy_recv[...]], axis=0)
    for index, ref in enumerate(refs[pieces:]):
        at = slice(index * tokens, (index + 1) * tokens)
        left = jnp.concatenate([piece[at] for piece in refs[:pieces]], axis=0)
        ref[...] = dot_rows(left, dy if index == 0 else x).astype(BF)


def shared_dx_kernel(blocks, halves, flag_ref, *refs):
    pieces = [refs[i * blocks : (i + 1) * blocks] for i in range(halves)]
    own_ref, oth_ref, *outs = refs[halves * blocks :]
    tokens = outs[0].shape[0]
    hidden, width = own_ref.shape[0] // 3, own_ref.shape[1]

    def collect(index):
        at = slice(index * tokens, (index + 1) * tokens)
        parts = [jnp.concatenate([ref[at] for ref in part], axis=0) for part in pieces]
        return jnp.concatenate(parts, axis=1)

    da, db = collect(1), collect(2)
    core = flag_ref[CORE]
    for place, ref in ((core, own_ref), (1 - core, oth_ref)):
        at = pl.ds(pl.multiple_of(place * width, 128), width)
        got = (dot(da, ref[:hidden]) + dot(db, ref[hidden : 2 * hidden])).astype(BF)
        parts = [got[j * tokens : (j + 1) * tokens] for j in range(blocks)]
        for j in range(blocks):
            outs[j][:, at] = parts[j]
        if len(outs) > blocks:
            outs[blocks][:, at] = jnp.where(flag_ref[ALIGNED] == 1, parts[1], parts[0])


def routed_kernel(pair, slices, waits, flag_ref, x_ref, dy_ref, gate_ref, up_ref, down_ref, *refs):
    new_gate, new_up, new_down, *refs = refs[waits:]
    outs, (acc, gate_acc, rows_x, rows_dy) = refs[:-4], refs[-4:]
    step = pl.program_id(0)
    slots, width = acc.shape
    piece = width // slices
    here = pl.ds(pl.multiple_of(flag_ref[LOCAL] * piece, 128), piece)
    there = pl.ds(pl.multiple_of((slices - 1 - flag_ref[LOCAL]) * piece, 128), piece)

    @pl.when(step == 0)
    def _():
        if pair:
            rows_x[:, here] = x_ref[:, :piece]
            rows_dy[:, here] = x_ref[:, piece:]
            rows_x[:, there] = dy_ref[:, :piece]
            rows_dy[:, there] = dy_ref[:, piece:]
        else:
            rows_x[...] = x_ref[...]
            rows_dy[...] = dy_ref[...]

    x = rows_x[...]
    dy = rows_dy[...]
    w_gate, w_up, w_down = gate_ref[0], up_ref[0], down_ref[0]
    pre_a = dot_cols(x, w_gate)
    pre_b = dot_cols(x, w_up)
    back_e = dot_cols(dy, w_down)
    sigm = jax.nn.sigmoid(pre_a)
    silu = pre_a * sigm
    hidden = silu * pre_b
    part = jnp.sum(back_e * hidden, axis=1, keepdims=True)
    grad_a = (back_e * pre_b * sigm * (1.0 + pre_a * (1.0 - sigm))).astype(BF)
    grad_b = (back_e * silu).astype(BF)
    row = dot(grad_a, w_gate) + dot(grad_b, w_up)
    new_gate[0] = dot_rows(grad_a, x).astype(BF)
    new_up[0] = dot_rows(grad_b, x).astype(BF)
    new_down[0] = dot_rows(hidden.astype(BF), dy).astype(BF)

    @pl.when(step == 0)
    def _():
        acc[...] = row
        gate_acc[...] = part

    @pl.when(step > 0)
    def _():
        acc[...] += row
        gate_acc[...] += part

    @pl.when(step == pl.num_programs(0) - 1)
    def _():
        lane = lax.broadcasted_iota(jnp.int32, (slots, 128), 1)
        sub = lax.broadcasted_iota(jnp.int32, (slots, 128), 0) % BLOCK
        spread = jnp.where(lane == sub, gate_acc[...], 0.0).reshape(slots // BLOCK, BLOCK, 128)
        line = jnp.sum(spread, axis=1, keepdims=True)
        line = jnp.broadcast_to(line, spread.shape).reshape(slots, 128)
        line = jnp.where(sub == GATE_ROW, line, 0.0)
        for index in range(slices):
            start = index * piece
            acc[:, start : start + 128] += line
        if pair:
            outs[0][...] = acc[:, here].astype(BF)
            outs[1][...] = acc[:, there].astype(BF)
        else:
            outs[0][...] = acc[...].astype(BF)


def combine_kernel(n_dp, flag_ref, expert_ref, slot_ref, gate_ref, rows_ref, *refs):
    dx_ref, gates_ref = refs[-2:]
    choices, tokens = slot_ref.shape
    slots = rows_ref.shape[0]
    line = lax.broadcasted_iota(jnp.int32, (slots, tokens), 0)
    sub = lax.broadcasted_iota(jnp.int32, (128, tokens), 0)
    pos = positions(expert_ref[...], slot_ref[...], n_dp)
    gate = gate_ref[...].astype(F32)
    rows = rows_ref[...]
    sel = jnp.zeros((slots, tokens), F32)
    for k in range(choices):
        at = pos[k : k + 1]
        sel = jnp.where(at == line, 1.0, sel)
        slot = at & (BLOCK - 1)
        pick = jnp.where((at >= 0) & (line == at - slot + GATE_ROW), 1.0, 0.0).astype(BF)
        found = dot_rows(rows[:, :128], pick)
        value = jnp.sum(jnp.where(sub == slot, found, 0.0), axis=0, keepdims=True)
        gates_ref[k : k + 1] = value / gate[k : k + 1]
    total = dot_rows(sel.astype(BF), rows)
    terms = refs[:-2]
    if len(terms) == 3:
        second = jnp.where(flag_ref[ALIGNED] == 1, terms[1][...], terms[2][...])
        total = total + terms[0][...].astype(F32) + second.astype(F32)
    else:
        total = total + terms[0][...].astype(F32)
    dx_ref[...] = total.astype(BF)


def add_kernel(own_ref, came_ref, out_ref):
    out_ref[...] = (own_ref[...].astype(F32) + came_ref[...].astype(F32)).astype(BF)


def total_kernel(flag_ref, own_ref, came_ref, next_ref, out_ref, pay_ref):
    total = (own_ref[...].astype(F32) + came_ref[...].astype(F32)).astype(BF)
    out_ref[...] = total
    pay_ref[...] = jnp.where(flag_ref[MIDDLE] == 1, total, next_ref[...])


def line_sum(value, n_node, depth):
    half = n_node // 2
    if n_node % 2:
        return lax.psum(value, "node")
    for k in range(half - 1):
        pairs = [(k, k + 1), (n_node - 1 - k, n_node - 2 - k)]
        got = lax.ppermute(value, "node", pairs)
        value = (value.astype(F32) + got.astype(F32)).astype(BF)
    got = lax.ppermute(value, "node", [(half - 1, half), (half, half - 1)])
    value = (value.astype(F32) + got.astype(F32)).astype(BF)
    for k in reversed(range(half - 1)):
        pairs = [(k + 1, k), (n_node - 2 - k, n_node - 1 - k)]
        got = lax.ppermute(value, "node", pairs)
        value = jnp.where(depth == k, got, value)
    return value


INWARD, CENTRE, OUTWARD = [(0, 1), (3, 2)], [(1, 2), (2, 1)], [(1, 0), (2, 3)]


class LineOfFour:
    def __init__(self, flags):
        self.flags = flags
        self.values, self.outer, self.sums, self.across, self.totals, self.ends = [], [], [], [], [], []
        self.last = []

    def add(self, values):
        self.values += values
        for value in self.values[len(self.outer) : 2]:
            self.outer.append(lax.ppermute(value, "node", INWARD))

    def step(self, kernel, name, operands, outs, after=(), held=(), flags=()):
        like = [shape(operands[0].shape, BF)] * outs
        got = call(kernel, like, operands, name, flags, self.last + list(after), held, LINE_BYTES)
        self.last = got[:1]
        return got

    def sum(self, after=()):
        now = len(self.sums)
        ahead = self.values[2:3] if now == 0 else []
        got = self.step(add_kernel, "line_sum", [self.values[now], self.outer[now]], 1, after, ahead)
        if ahead:
            self.values[2] = got[1]
            self.outer.append(lax.ppermute(got[1], "node", INWARD))
        self.sums.append(got[0])
        self.across.append(lax.ppermute(got[0], "node", CENTRE))

    def total(self, after=(), held=()):
        back = len(self.totals)
        operands = [self.sums[back], self.across[back]]
        waits = list(after) + (self.ends[back - 2 : back - 1] if back > 1 else [])
        if back + 3 < len(self.values):
            operands.append(self.values[back + 3])
            got = self.step(total_kernel, "line_total", operands, 2, waits, held, [self.flags])
            came = lax.ppermute(got[1], "node", INWARD + OUTWARD)
            self.outer.append(came)
            held = got[2:]
        else:
            got = self.step(add_kernel, "line_total", operands, 1, waits, held)
            came = lax.ppermute(got[0], "node", OUTWARD)
            held = got[1:]
        self.totals.append(got[0])
        self.ends.append(came)
        return list(held)

    def finish(self, middle):
        while len(self.sums) < len(self.values):
            self.sum()
        while len(self.totals) < len(self.values):
            self.total()
        return [jnp.where(middle, a, b) for a, b in zip(self.totals, self.ends)]


def on_device(
    layer_input,
    grad_out,
    gate_values,
    route_expert,
    route_slot,
    shared_gate,
    shared_up,
    shared_down,
    expert_gate,
    expert_up,
    expert_down,
):
    n_node = lax.axis_size("node")
    n_local = lax.axis_size("local")
    n_dp = lax.axis_size("dp")
    outer = n_dp // 2
    groups = n_node * n_dp
    slots = groups * BLOCK
    tokens, feat = layer_input.shape
    hidden_s, width = shared_gate.shape
    hidden_r, model = expert_gate.shape[1:]
    local = lax.axis_index("local")
    dp = lax.axis_index("dp")
    node = lax.axis_index("node")
    row, core = dp // 2, dp % 2
    paired = n_local == 2 and outer == 2
    middle = (node == 1) | (node == 2)
    flags = jnp.stack([core, row == local, local, middle]).astype(jnp.int32)

    swap_core = [(d, d ^ 1) for d in range(n_dp)]

    def outer_shift(step):
        return [(d, (d + 2 * step) % n_dp) for d in range(n_dp)]

    def at(l, y, c):
        return l * n_dp + 2 * y + c

    straight, diagonal = [], []
    if paired:
        for l in range(2):
            for c in range(2):
                straight.append((at(l, l, c), at(1 - l, l, c)))
                straight.append((at(l, 1 - l, c), at(l, l, c)))
                diagonal.append((at(l, 1 - l, c), at(1 - l, l, c)))
    backwards = [(b, a) for a, b in straight]

    def core_swap(value):
        return lax.ppermute(value, "dp", swap_core)

    def feature_blocks(own):
        if paired:
            first = lax.ppermute(own, ("local", "dp"), straight)
            second = lax.ppermute(own, ("local", "dp"), diagonal)
            return [own, first, second]
        full = lax.all_gather(own, "local", axis=1, tiled=True)
        found = [lax.dynamic_slice_in_dim(full, row * 2 * width, 2 * width, axis=1)]
        for step in range(1, outer):
            there = (row + outer - step) % outer
            piece = lax.dynamic_slice_in_dim(full, there * 2 * width, 2 * width, axis=1)
            found.append(lax.ppermute(piece, "dp", outer_shift(outer - step)))
        return found

    def gather_groups(value):
        near = [value]
        for step in range(1, outer):
            near.append(lax.ppermute(value, "dp", outer_shift(outer - step)))
        return near + [core_swap(v) for v in near]

    gate_values, route_expert, route_slot = gate_values.T, route_expert.T, route_slot.T
    x_blocks = feature_blocks(layer_input)
    dy_blocks = feature_blocks(grad_out)
    weights = [shared_gate, shared_up, shared_down]
    (shared,) = call(pack_kernel, [shape((3 * hidden_s, width), BF)], [far(v) for v in weights], "pack_weights")
    shared_oth = core_swap(shared)

    (send_rows,) = call(
        functools.partial(select_kernel, n_dp),
        [shape((slots, 2 * feat), BF)],
        [far(v) for v in (route_expert, route_slot, gate_values, layer_input, grad_out)],
        "select_rows",
        after=[shared_oth],
    )
    back_rows = lax.all_to_all(
        send_rows.reshape(groups, BLOCK, 2 * feat),
        ("node", "dp"),
        split_axis=0,
        concat_axis=0,
        tiled=True,
    ).reshape(slots, 2 * feat)

    halves = 2 if hidden_s % 256 == 0 else 1
    part = hidden_s // halves

    def partial(blocks, weight, oth, first, mats, name, after):
        x_keep, x_send, *got = call(
            functools.partial(product_kernel, len(blocks), outer, first, mats),
            [shape((outer * tokens, width), BF)] * 2
            + [shape((mats * tokens, hidden_s), F32)]
            + [shape((mats * tokens, hidden_s), BF)] * (outer - 1),
            ([far(blocks[0])] + blocks[1:] if paired else blocks) + [weight, oth],
            name,
            [flags],
            after,
            far_outs=(0, 1),
        )
        sums = [got[0]]
        for step in range(1, outer):
            sums.append(lax.ppermute(got[step], "dp", outer_shift(step)))
        return x_keep, core_swap(x_send), sums

    x_keep, x_recv, ab_sums = partial(x_blocks, shared, shared_oth, 0, 2, "shared_ab", [send_rows])
    dy_keep, dy_recv, e_sums = partial(
        dy_blocks, shared, shared_oth, 2, 1, "shared_e", ab_sums[:1]
    )
    values = call(
        functools.partial(slope_kernel, len(e_sums)),
        [shape((3 * tokens, part), BF)] * halves,
        ab_sums + e_sums,
        "shared_slopes",
        after=[x_recv, dy_recv],
    )
    pair = n_local == 2
    swap_local = [(0, 1), (1, 0)]
    if pair:
        row_operands = [back_rows, lax.ppermute(back_rows, "local", swap_local)]
    else:
        row_operands = [
            lax.all_gather(back_rows[:, :feat], "local", axis=1, tiled=True),
            lax.all_gather(back_rows[:, feat:], "local", axis=1, tiled=True),
        ]

    def weight_grads(pieces, after):
        rows = [x_keep, x_recv, dy_keep, dy_recv]
        return call(
            functools.partial(weight_grad_kernel, len(pieces)),
            [shape((part, width), BF)] * 3,
            [far(v) for v in rows] + pieces,
            "shared_weight_grads",
            after=after,
        )

    line = LineOfFour(flags) if n_node == 4 else None
    slopes = [gather_groups(values[0])]
    parts = weight_grads(slopes[0], row_operands[1:])
    if line:
        line.add(parts)
        parts = line.values

    row_outs = [shape((slots, feat), BF)] * 2 if pair else [shape((slots, model), BF)]
    waits = parts[:1]
    block = hidden_r // 2 if hidden_r % 128 == 0 else hidden_r
    tile = pl.BlockSpec((1, block, model), lambda i: (0, i, 0))
    experts = [far(v)[1] for v in (expert_gate, expert_up, expert_down)]
    new_gate, new_up, new_down, *rows_out = pl.pallas_call(
        functools.partial(routed_kernel, pair, n_local, len(waits)),
        grid=(hidden_r // block,),
        out_shape=[pltpu.HBM((1, hidden_r, model), BF)] * 3 + row_outs,
        in_specs=[SMEM]
        + [VMEM] * len(row_operands)
        + [tile, tile, tile]
        + [ANY] * len(waits),
        out_specs=[tile, tile, tile] + [VMEM] * len(row_outs),
        scratch_shapes=[
            pltpu.VMEM((slots, model), F32),
            pltpu.VMEM((slots, 1), F32),
            pltpu.VMEM((slots, model), BF),
            pltpu.VMEM((slots, model), BF),
        ],
        compiler_params=pltpu.CompilerParams(vmem_limit_bytes=VMEM_BYTES),
        cost_estimate=pl.CostEstimate(flops=0, bytes_accessed=0, transcendentals=0),
        name="routed_expert",
    )(flags, *row_operands, *experts, *waits)
    if pair:
        mine, gone = rows_out
        came = lax.ppermute(gone, "local", swap_local)
        row_sum = (mine.astype(F32) + came.astype(F32)).astype(BF)
    else:
        row_sum = lax.psum_scatter(rows_out[0], "local", scatter_dimension=1, tiled=True)
    for value in values[1:]:
        (value,) = call(lambda: None, [], [], "hold", after=slopes[-1][1:outer], held=[value])
        slopes.append(gather_groups(value))
        more = weight_grads(slopes[-1], rows_out[:1])
        if line:
            line.add(more)
        else:
            parts = parts + more
    if line:
        line.sum(rows_out[:1])
        line.sum()
        line.total()
    dx_blocks = call(
        functools.partial(shared_dx_kernel, outer, halves),
        [shape((tokens, 2 * width), BF)] * (outer + (1 if paired else 0)),
        sum((pieces[:outer] for pieces in slopes), []) + [shared, shared_oth],
        "shared_dx",
        [flags],
        line.last if line else (),
    )
    if line:
        line.sum(dx_blocks[:1])
        dx_blocks = line.total(held=dx_blocks)
        line.sum()
        line.total()
        line.sum()
        (row_sum,) = line.total(held=[row_sum])
    home = lax.all_to_all(
        row_sum.reshape(groups, BLOCK, feat),
        ("node", "dp"),
        split_axis=0,
        concat_axis=0,
        tiled=True,
    ).reshape(slots, feat)
    if line:
        line.sum()
        line.total()
    if paired:
        mine, other, straight_pay = dx_blocks
        first = lax.ppermute(straight_pay, ("local", "dp"), backwards)
        second = lax.ppermute(other, ("local", "dp"), diagonal)
        dx_terms = [first, mine, second]
    else:
        full = jnp.zeros((tokens, model), BF)
        for step, piece in enumerate(dx_blocks):
            if step:
                piece = lax.ppermute(piece, "dp", outer_shift(step))
            there = (row + outer - step) % outer
            full = lax.dynamic_update_slice_in_dim(full, piece, there * 2 * width, axis=1)
        dx_terms = [lax.psum_scatter(full, "local", scatter_dimension=1, tiled=True)]
    grad_x, grad_gates = call(
        functools.partial(combine_kernel, n_dp),
        [shape((tokens, feat), BF), shape(route_slot.shape, F32)],
        [far(v) for v in [route_expert, route_slot, gate_values, home] + dx_terms],
        "combine",
        [flags],
        line.last if line else (),
        far_outs=(0, 1),
    )
    if line:
        line.total([grad_x])
        parts = line.finish(middle)
    else:
        depth = jnp.minimum(node, n_node - 1 - node)
        parts = [line_sum(value, n_node, depth) for value in parts]
    grad_down, grad_gate, grad_up = (
        jnp.concatenate(parts[i::3], axis=0) if halves > 1 else parts[i] for i in range(3)
    )
    if n_local > 2:
        grad_gates = lax.psum(jnp.where(local == 0, grad_gates, 0.0), "local")
    return grad_x, grad_gates.T, grad_gate, grad_up, grad_down, new_gate, new_up, new_down


def solution(mesh):
    tokens = P(("node", "dp"), "local")
    choices = P(("node", "dp"), None)
    shared = P("local", "dp")
    expert = P(("node", "dp"), "local", None)
    return jax.shard_map(
        on_device,
        mesh=mesh,
        in_specs=(tokens, tokens, choices, choices, choices) + (shared,) * 3 + (expert,) * 3,
        out_specs=(tokens, choices) + (shared,) * 3 + (expert,) * 3,
        check_vma=False,
    )
```

time: 431 us -> 181 us (0.42)
  waiting for transfers between devices: 217 us -> 60 us
  blocking collectives: 59.9 us -> 0 us
  local copies, waits for them, and re-layouts: 58.1 us -> 7.76 us
  matrix products: 44.7 us -> 0 us
  Pallas kernels: 0 us -> 36.9 us
  starting transfers between devices: 33.2 us -> 65.4 us
  between operations: 14.5 us -> 1.06 us
  other arithmetic: 0.93 us -> 8.5 us
    all_gather x3 -> x0, waiting for transfers between devices: 75.4 us -> none  [the longest x1 30.4 us: on_device(): lax.all_gather(shared_down, 'dp', axis=1, tiled=True)]
    psum x1 -> x0, waiting for transfers between devices: 66.3 us -> none  [on_device(): lax.psum(sum_gate.astype(jnp.bfloat16), 'node').astype(jnp.float32)]
    ppermute x0 -> x34, waiting for transfers between devices: none -> 55.8 us  [the longest x3 19.8 us: total(): came = lax.ppermute(got[0], 'node', OUTWARD)]
    all_gather x4 -> x0, blocking collectives: 55 us -> none  [the longest x1 28.8 us: on_device(): lax.all_gather(grad_a, 'local', axis=1, tiled=True)]
    ppermute x0 -> x34, starting transfers between devices: none -> 51 us  [the longest x3 12.5 us: total(): came = lax.ppermute(got[1], 'node', INWARD + OUTWARD)]
    dot_general x19 -> x0, matrix products: 44.7 us -> none  [the longest x6 17.4 us: contract_rows(): lax.dot_general(left, right, (((0,), (0,)), ((), ())), preferred_element_...]
    all_to_all x7 -> x2, waiting for transfers between devices: 47.5 us -> 4.18 us  [the longest x1 4.18 us: on_device(): lax.all_to_all(row_sum.reshape(groups, BLOCK, feat), ('node', 'dp'), spli...]
    pallas_call x0 -> x23, Pallas kernels: none -> 36.9 us  [the longest x22 26.4 us: call(): pl.pallas_call(body, grid=(1,), out_shape=[pltpu.HBM(v.shape, v.dtype) if...]
  transfers between devices with their start and end apart: 15 -> 36, of which waited for: 10 -> 11; matrix products, arithmetic and copies ran while one was open for 20% -> 4% of each run, Pallas kernels for 0% -> 17%
where the time goes in v1:
time: 181 us; the launch traced here: 180 us
  starting transfers between devices  65.4 us (36%)
  waiting for transfers between devices  60 us (33%)
  Pallas kernels  36.9 us (20%)
  other arithmetic  8.5 us (5%)
  local copies, waits for them, and re-layouts  7.76 us (4%)
    pallas_call x22, Pallas kernels, call(): pl.pallas_call(body, grid=(1,), out_shape=[pltpu.HBM(v.shape, v.dtype) if...  26.4 us
    ppermute x3, waiting for transfers between devices, total(): came = lax.ppermute(got[0], 'node', OUTWARD)  19.8 us
    ppermute x3, starting transfers between devices, total(): came = lax.ppermute(got[1], 'node', INWARD + OUTWARD)  12.5 us
    ppermute x2, waiting for transfers between devices, feature_blocks(): first = lax.ppermute(own, ('local', 'dp'), straight)  10.7 us
    pallas_call x1, Pallas kernels, on_device(): pl.pallas_call(functools.partial(routed_kernel, pair, n_local, len(waits)...  10.5 us
    unnamed x40, local copies, waits for them, and re-layouts  7.76 us
    all_to_all x1, starting transfers between devices, on_device(): lax.all_to_all(send_rows.reshape(groups, BLOCK, 2 * feat), ('node', 'dp')...  7.35 us
    ppermute x2, waiting for transfers between devices, gather_groups(): near.append(lax.ppermute(value, 'dp', outer_shift(outer - step)))  7.05 us
  transfers between devices with their start and end apart: 36, of which 11 were waited for; matrix products, arithmetic and copies ran while one was open for 4% of the time, Pallas kernels for 17%

profile of v1, /device:TPU:0, one launch (start us, length us, event | category | flops | bytes accessed | tf_op | source)
XLA Modules:
  0.0 179.6 jit_solution(12590471212374550244)
XLA Ops:
  3.2 5.0 %collective-permute-done.2.refs_5_.refs_6_ = bf16[2304,640]{1,0:T(8,128)(2,1)S(1)} collective-permute-done((bf16[2304,640]{1,0:T(8,128)(2,1)S(1)}, bf16[2304,640]{1,0:T(8,128)(2,1)S(1)}, u32[]{:S(2)}, u32[]{:S(2)}) %collective-permute-start.2) | collective-permute-done | bytes 2949152 | tf_op jit(solution)/shard_map/ppermute | solution.py:403
  11.1 7.4 %all-to-all-start = ((bf16[16,8,2560]{2,1,0:T(8,128)(2,1)}), bf16[16,8,2560]{2,1,0:T(8,128)(2,1)}, u32[]{:S(2)}, u32[]{:S(2)}) async-start(bf16[16,8,2560]{2,1,0:T(8,128)(2,1)} %bitcast.12), calls=%async_computation | async-start | bytes 1310720 | tf_op jit(solution)/shard_map/all_to_all | solution.py:438
  21.4 2.5 %collective-permute-start.4 = (bf16[128,1280]{1,0:T(8,128)(2,1)}, bf16[128,1280]{1,0:T(8,128)(2,1)S(1)}, u32[]{:S(2)}, u32[]{:S(2)}) collective-permute-start(bf16[128,1280]{1,0:T(8,128)(2,1)} %refs_1_.5), channel_id=1, source_target_pairs={{0,4},{2,0},{1,5},{3,1},{6,2},{4,6},{7,3},{5,7},{8,12},{10,8},{9,1... | collective-permute-start | bytes 983048 | tf_op jit(solution)/shard_map/ppermute | solution.py:407
  25.4 10.7 %collective-permute-done.refs_2_ = bf16[128,1280]{1,0:T(8,128)(2,1)} collective-permute-done((bf16[128,1280]{1,0:T(8,128)(2,1)}, bf16[128,1280]{1,0:T(8,128)(2,1)}, u32[]{:S(2)}, u32[]{:S(2)}) %collective-permute-start) | collective-permute-done | bytes 327712 | tf_op jit(solution)/shard_map/ppermute | solution.py:407
  39.1 3.4 %shared_ab.1 = (bf16[256,640]{1,0:T(8,128)(2,1)}, bf16[256,640]{1,0:T(8,128)(2,1)}, f32[256,768]{1,0:T(8,128)S(1)}, bf16[256,768]{1,0:T(8,128)(2,1)}) custom-call(s32[4]{0:T(128)S(1)} %pad_add_fusion.refs_0_.flag_ref, bf16[128,1280]{1,0:T(8,128)(2,1)} %refs_1_.4, bf16[128,1280]{1,0:T(8,128)(2,1)} %collective-permute-done.refs_2_, ...), custom_call_target="tpu_custom_call" | custom-call | tf_op jit(solution)/shard_map/shared_ab/pallas_call | solution.py:54
  42.4 2.3 %collective-permute-start.7 = (bf16[256,768]{1,0:T(8,128)(2,1)}, bf16[256,768]{1,0:T(8,128)(2,1)}, u32[]{:S(2)}, u32[]{:S(2)}) collective-permute-start(bf16[256,768]{1,0:T(8,128)(2,1)} %get-tuple-element.52), channel_id=1, source_target_pairs={{0,2},{1,3},{2,0},{3,1},{4,6},{5,7},{6,4},{7,5},{8,10},{9,11},{10,... | collective-permute-start | bytes 1179656 | tf_op jit(solution)/shard_map/ppermute | solution.py:463
  44.8 2.6 %shared_e.1 = (bf16[256,640]{1,0:T(8,128)(2,1)}, bf16[256,640]{1,0:T(8,128)(2,1)}, f32[128,768]{1,0:T(8,128)S(1)}, bf16[128,768]{1,0:T(8,128)(2,1)}) custom-call(s32[4]{0:T(128)S(1)} %pad_add_fusion.refs_0_.flag_ref, bf16[128,1280]{1,0:T(8,128)(2,1)} %refs_1_.5, bf16[128,1280]{1,0:T(8,128)(2,1)S(1)} %collective-permute-done.4.refs_2_, ...), custom_call_target="tpu_custom_call" | custom-call | tf_op jit(solution)/shard_map/shared_e/pallas_call | solution.py:54
  48.9 2.3 %collective-permute-start.13 = (bf16[128,2560]{1,0:T(8,128)(2,1)}, bf16[128,2560]{1,0:T(8,128)(2,1)S(1)}, u32[]{:S(2)}, u32[]{:S(2)}) collective-permute-start(bf16[128,2560]{1,0:T(8,128)(2,1)} %bitcast.8.x_ref), channel_id=1, source_target_pairs={{0,4},{4,0},{1,5},{5,1},{2,6},{6,2},{3,7},{7,3},{8,12},{12,8},{9,1... | collective-permute-start | bytes 1966088 | tf_op jit(solution)/shard_map/ppermute | solution.py:480
  51.2 5.2 %collective-permute-done.8.refs_3_ = bf16[128,768]{1,0:T(8,128)(2,1)S(1)} collective-permute-done((bf16[128,768]{1,0:T(8,128)(2,1)}, bf16[128,768]{1,0:T(8,128)(2,1)S(1)}, u32[]{:S(2)}, u32[]{:S(2)}) %collective-permute-start.8) | collective-permute-done | bytes 196640 | tf_op jit(solution)/shard_map/ppermute | solution.py:463
  61.3 7.0 %collective-permute-done.9.refs_0_.refs_5_.refs_2_ = bf16[384,384]{1,0:T(8,128)(2,1)S(1)} collective-permute-done((bf16[384,384]{1,0:T(8,128)(2,1)S(1)}, bf16[384,384]{1,0:T(8,128)(2,1)S(1)}, u32[]{:S(2)}, u32[]{:S(2)}) %collective-permute-start.9) | collective-permute-done | bytes 294944 | tf_op jit(solution)/shard_map/ppermute | solution.py:421
  69.9 2.4 %shared_weight_grads.2 = (bf16[384,640]{1,0:T(8,128)(2,1)S(1)}, bf16[384,640]{1,0:T(8,128)(2,1)S(1)}, bf16[384,640]{1,0:T(8,128)(2,1)S(1)}) custom-call(bf16[256,640]{1,0:T(8,128)(2,1)} %get-tuple-element.47.refs_0_, bf16[256,640]{1,0:T(8,128)(2,1)} %collective-permute-done.3.refs_4_.refs_1_, bf16[256,640]{1,0:T(8,128)(2,1)} %get-tuple-element.50.refs_2_, ...), custom_call_target="tpu_custom_call" | custom-call | tf_op jit(solution)/shard_map/shared_weight_grads/pallas_call | solution.py:54
  72.3 3.1 %collective-permute-start.16 = (bf16[384,640]{1,0:T(8,128)(2,1)S(1)}, bf16[384,640]{1,0:T(8,128)(2,1)S(1)}, u32[]{:S(2)}, u32[]{:S(2)}) collective-permute-start(bf16[384,640]{1,0:T(8,128)(2,1)S(1)} %get-tuple-element.57.refs_0_), channel_id=1, source_target_pairs={{0,8},{24,16},{1,9},{25,17},{2,10},{26,18},{3,11},{27,19},{4,12},{... | collective-permute-start | bytes 1474568 | tf_op jit(solution)/shard_map/ppermute | solution.py:311
  77.8 10.5 %routed_expert.1 = (bf16[1,384,2560]{2,1,0:T(8,128)(2,1)}, bf16[1,384,2560]{2,1,0:T(8,128)(2,1)}, bf16[1,384,2560]{2,1,0:T(8,128)(2,1)}, bf16[128,1280]{1,0:T(8,128)(2,1)S(1)}, bf16[128,1280]{1,0:T(8,128)(2,1)S(1)}) custom-call(s32[4]{0:T(128)S(1)} %pad_add_fusion.refs_0_.flag_ref, bf16[128,2560]{1,0:T(8,128)(2,1)} %bitcast.8.x_ref, ...), custom_call_target="tpu_custom_call" | custom-call | tf_op jit(solution)/shard_map/routed_expert/pallas_call | solution.py:509
  89.7 6.0 %collective-permute-start.21 = (bf16[384,640]{1,0:T(8,128)(2,1)S(1)}, bf16[384,640]{1,0:T(8,128)(2,1)S(1)}, u32[]{:S(2)}, u32[]{:S(2)}) collective-permute-start(bf16[384,640]{1,0:T(8,128)(2,1)S(1)} %get-tuple-element.65.refs_0_), channel_id=1, source_target_pairs={{0,8},{24,16},{1,9},{25,17},{2,10},{26,18},{3,11},{27,19},{4,12},{... | collective-permute-start | bytes 1474568 | tf_op jit(solution)/shard_map/ppermute | solution.py:325
  98.4 2.4 %shared_weight_grads.3 = (bf16[384,640]{1,0:T(8,128)(2,1)S(1)}, bf16[384,640]{1,0:T(8,128)(2,1)S(1)}, bf16[384,640]{1,0:T(8,128)(2,1)S(1)}) custom-call(bf16[256,640]{1,0:T(8,128)(2,1)} %get-tuple-element.47.refs_0_, bf16[256,640]{1,0:T(8,128)(2,1)} %collective-permute-done.3.refs_4_.refs_1_, bf16[256,640]{1,0:T(8,128)(2,1)} %get-tuple-element.50.refs_2_, ...), custom_call_target="tpu_custom_call" | custom-call | tf_op jit(solution)/shard_map/shared_weight_grads/pallas_call | solution.py:54
  101.6 5.6 %collective-permute-start.19 = (bf16[384,640]{1,0:T(8,128)(2,1)S(1)}, bf16[384,640]{1,0:T(8,128)(2,1)S(1)}, u32[]{:S(2)}, u32[]{:S(2)}) collective-permute-start(bf16[384,640]{1,0:T(8,128)(2,1)S(1)} %get-tuple-element.63), channel_id=1, source_target_pairs={{0,8},{24,16},{8,0},{16,24},{1,9},{25,17},{9,1},{17,25},{2,10},{26... | collective-permute-start | bytes 1474568 | tf_op jit(solution)/shard_map/ppermute | solution.py:336
  108.5 2.8 %shared_dx.1 = (bf16[128,1280]{1,0:T(8,128)(2,1)S(1)}, bf16[128,1280]{1,0:T(8,128)(2,1)}, bf16[128,1280]{1,0:T(8,128)(2,1)}) custom-call(s32[4]{0:T(128)S(1)} %pad_add_fusion.refs_0_.flag_ref, bf16[384,384]{1,0:T(8,128)(2,1)S(1)} %get-tuple-element.55.refs_4_.refs_1_, bf16[384,384]{1,0:T(8,128)(2,1)S(1)} %collective-permute-done.9.refs_0_.refs_5_.refs_2_, ...), custom_call_target="tpu_custom_call" | custom-call | tf_op jit(solution)/shard_map/shared_dx/pallas_call | solution.py:54
  115.1 4.2 %collective-permute-done.19.refs_1_.refs_5_ = bf16[384,640]{1,0:T(8,128)(2,1)S(1)} collective-permute-done((bf16[384,640]{1,0:T(8,128)(2,1)S(1)}, bf16[384,640]{1,0:T(8,128)(2,1)S(1)}, u32[]{:S(2)}, u32[]{:S(2)}) %collective-permute-start.19) | collective-permute-done | bytes 491552 | tf_op jit(solution)/shard_map/ppermute | solution.py:336
  124.2 4.7 %collective-permute-start.29 = (bf16[384,640]{1,0:T(8,128)(2,1)}, bf16[384,640]{1,0:T(8,128)(2,1)S(1)}, u32[]{:S(2)}, u32[]{:S(2)}) collective-permute-start(bf16[384,640]{1,0:T(8,128)(2,1)} %get-tuple-element.79), channel_id=1, source_target_pairs={{0,8},{24,16},{8,0},{16,24},{1,9},{25,17},{9,1},{17,25},{2,10},{26... | collective-permute-start | bytes 1474568 | tf_op jit(solution)/shard_map/ppermute | solution.py:336
  133.3 7.0 %all-to-all-start.1 = ((bf16[16,8,1280]{2,1,0:T(8,128)(2,1)}), bf16[16,8,1280]{2,1,0:T(8,128)(2,1)}, u32[]{:S(2)}, u32[]{:S(2)}) async-start(bf16[16,8,1280]{2,1,0:T(8,128)(2,1)} %bitcast.9), calls=%async_computation.1 | async-start | bytes 655360 | tf_op jit(solution)/shard_map/all_to_all | solution.py:561
  145.4 8.5 %collective-permute-done.32.refs_4_ = bf16[384,640]{1,0:T(8,128)(2,1)S(1)} collective-permute-done((bf16[384,640]{1,0:T(8,128)(2,1)S(1)}, bf16[384,640]{1,0:T(8,128)(2,1)S(1)}, u32[]{:S(2)}, u32[]{:S(2)}) %collective-permute-start.32) | collective-permute-done | bytes 491552 | tf_op jit(solution)/shard_map/ppermute | solution.py:341
  154.8 4.2 %all-to-all-done.1 = bf16[16,8,1280]{2,1,0:T(8,128)(2,1)} async-done(((bf16[16,8,1280]{2,1,0:T(8,128)(2,1)}), bf16[16,8,1280]{2,1,0:T(8,128)(2,1)}, u32[]{:S(2)}, u32[]{:S(2)}) %all-to-all-start.1) | async-done | bytes 327712 | tf_op jit(solution)/shard_map/all_to_all | solution.py:561
  159.0 2.5 %combine.1 = (bf16[128,1280]{1,0:T(8,128)(2,1)}, f32[6,128]{1,0:T(8,128)}) custom-call(s32[4]{0:T(128)S(1)} %pad_add_fusion.refs_0_.flag_ref, s32[6,128]{1,0:T(8,128)} %bitcast.14, s32[6,128]{1,0:T(8,128)} %bitcast.16, bf16[6,128]{1,0:T(8,128)(2,1)} %bitcast.18, bf16[128,1280]{1,0:T(8,128)(2,1)} %bitcast.10.refs_4_, ...), custom_call_target="tpu_custom_call" | custom-call | tf_op jit(solution)/shard_map/combine/pallas_call | solution.py:54
  167.2 11.2 %collective-permute-done.33 = bf16[384,640]{1,0:T(8,128)(2,1)S(1)} collective-permute-done((bf16[384,640]{1,0:T(8,128)(2,1)S(1)}, bf16[384,640]{1,0:T(8,128)(2,1)S(1)}, u32[]{:S(2)}, u32[]{:S(2)}) %collective-permute-start.33) | collective-permute-done | bytes 491552 | tf_op jit(solution)/shard_map/ppermute | solution.py:341
  (122 shorter events, 55.0 us)
Async XLA Ops:
  11.1 37.8 %all-to-all-start = ((bf16[16,8,2560]{2,1,0:T(8,128)(2,1)}), bf16[16,8,2560]{2,1,0:T(8,128)(2,1)}, u32[]{:S(2)}, u32[]{:S(2)}) async-start(bf16[16,8,2560]{2,1,0:T(8,128)(2,1)} %bitcast.12), calls=%async_computation | async-start | bytes 1310720 | tf_op jit(solution)/shard_map/all_to_all | solution.py:438
  18.4 17.7 %collective-permute-start = (bf16[128,1280]{1,0:T(8,128)(2,1)}, bf16[128,1280]{1,0:T(8,128)(2,1)}, u32[]{:S(2)}, u32[]{:S(2)}) collective-permute-start(bf16[128,1280]{1,0:T(8,128)(2,1)} %refs_1_.4), channel_id=1, source_target_pairs={{0,4},{2,0},{1,5},{3,1},{6,2},{4,6},{7,3},{5,7},{8,12},{10,8},{9,1... | collective-permute-start | bytes 983048 | tf_op jit(solution)/shard_map/ppermute | solution.py:407
  20.0 16.2 %collective-permute-start.1 = (bf16[128,1280]{1,0:T(8,128)(2,1)}, bf16[128,1280]{1,0:T(8,128)(2,1)}, u32[]{:S(2)}, u32[]{:S(2)}) collective-permute-start(bf16[128,1280]{1,0:T(8,128)(2,1)} %refs_1_.4), channel_id=1, source_target_pairs={{2,4},{3,5},{4,2},{5,3},{10,12},{11,13},{12,10},{13,11},{18,20},{1... | collective-permute-start | bytes 983048 | tf_op jit(solution)/shard_map/ppermute | solution.py:408
  21.4 23.4 %collective-permute-start.4 = (bf16[128,1280]{1,0:T(8,128)(2,1)}, bf16[128,1280]{1,0:T(8,128)(2,1)S(1)}, u32[]{:S(2)}, u32[]{:S(2)}) collective-permute-start(bf16[128,1280]{1,0:T(8,128)(2,1)} %refs_1_.5), channel_id=1, source_target_pairs={{0,4},{2,0},{1,5},{3,1},{6,2},{4,6},{7,3},{5,7},{8,12},{10,8},{9,1... | collective-permute-start | bytes 983048 | tf_op jit(solution)/shard_map/ppermute | solution.py:407
  23.9 20.8 %collective-permute-start.5 = (bf16[128,1280]{1,0:T(8,128)(2,1)}, bf16[128,1280]{1,0:T(8,128)(2,1)}, u32[]{:S(2)}, u32[]{:S(2)}) collective-permute-start(bf16[128,1280]{1,0:T(8,128)(2,1)} %refs_1_.5), channel_id=1, source_target_pairs={{2,4},{3,5},{4,2},{5,3},{10,12},{11,13},{12,10},{13,11},{18,20},{1... | collective-permute-start | bytes 983048 | tf_op jit(solution)/shard_map/ppermute | solution.py:408
  42.4 14.0 %collective-permute-start.7 = (bf16[256,768]{1,0:T(8,128)(2,1)}, bf16[256,768]{1,0:T(8,128)(2,1)}, u32[]{:S(2)}, u32[]{:S(2)}) collective-permute-start(bf16[256,768]{1,0:T(8,128)(2,1)} %get-tuple-element.52), channel_id=1, source_target_pairs={{0,2},{1,3},{2,0},{3,1},{4,6},{5,7},{6,4},{7,5},{8,10},{9,11},{10,... | collective-permute-start | bytes 1179656 | tf_op jit(solution)/shard_map/ppermute | solution.py:463
  48.9 21.0 %collective-permute-start.13 = (bf16[128,2560]{1,0:T(8,128)(2,1)}, bf16[128,2560]{1,0:T(8,128)(2,1)S(1)}, u32[]{:S(2)}, u32[]{:S(2)}) collective-permute-start(bf16[128,2560]{1,0:T(8,128)(2,1)} %bitcast.8.x_ref), channel_id=1, source_target_pairs={{0,4},{4,0},{1,5},{5,1},{2,6},{6,2},{3,7},{7,3},{8,12},{12,8},{9,1... | collective-permute-start | bytes 1966088 | tf_op jit(solution)/shard_map/ppermute | solution.py:480
  72.3 16.0 %collective-permute-start.16 = (bf16[384,640]{1,0:T(8,128)(2,1)S(1)}, bf16[384,640]{1,0:T(8,128)(2,1)S(1)}, u32[]{:S(2)}, u32[]{:S(2)}) collective-permute-start(bf16[384,640]{1,0:T(8,128)(2,1)S(1)} %get-tuple-element.57.refs_0_), channel_id=1, source_target_pairs={{0,8},{24,16},{1,9},{25,17},{2,10},{26,18},{3,11},{27,19},{4,12},{... | collective-permute-start | bytes 1474568 | tf_op jit(solution)/shard_map/ppermute | solution.py:311
  75.4 13.8 %collective-permute-start.10 = (bf16[384,384]{1,0:T(8,128)(2,1)S(1)}, bf16[384,384]{1,0:T(8,128)(2,1)S(1)}, u32[]{:S(2)}, u32[]{:S(2)}) collective-permute-start(bf16[384,384]{1,0:T(8,128)(2,1)S(1)} %hold.1.refs_4_.refs_3_), channel_id=1, source_target_pairs={{0,2},{1,3},{2,0},{3,1},{4,6},{5,7},{6,4},{7,5},{8,10},{9,11},{10,... | collective-permute-start | bytes 884744 | tf_op jit(solution)/shard_map/ppermute | solution.py:421
  76.5 21.0 %collective-permute-start.18 = (bf16[384,640]{1,0:T(8,128)(2,1)S(1)}, bf16[384,640]{1,0:T(8,128)(2,1)S(1)}, u32[]{:S(2)}, u32[]{:S(2)}) collective-permute-start(bf16[384,640]{1,0:T(8,128)(2,1)S(1)} %get-tuple-element.62.refs_0_), channel_id=1, source_target_pairs={{0,8},{24,16},{1,9},{25,17},{2,10},{26,18},{3,11},{27,19},{4,12},{... | collective-permute-start | bytes 1474568 | tf_op jit(solution)/shard_map/ppermute | solution.py:311
  89.7 21.6 %collective-permute-start.21 = (bf16[384,640]{1,0:T(8,128)(2,1)S(1)}, bf16[384,640]{1,0:T(8,128)(2,1)S(1)}, u32[]{:S(2)}, u32[]{:S(2)}) collective-permute-start(bf16[384,640]{1,0:T(8,128)(2,1)S(1)} %get-tuple-element.65.refs_0_), channel_id=1, source_target_pairs={{0,8},{24,16},{1,9},{25,17},{2,10},{26,18},{3,11},{27,19},{4,12},{... | collective-permute-start | bytes 1474568 | tf_op jit(solution)/shard_map/ppermute | solution.py:325
  97.6 14.5 %collective-permute-start.20 = (bf16[384,640]{1,0:T(8,128)(2,1)S(1)}, bf16[384,640]{1,0:T(8,128)(2,1)S(1)}, u32[]{:S(2)}, u32[]{:S(2)}) collective-permute-start(bf16[384,640]{1,0:T(8,128)(2,1)S(1)} %line_sum.7.refs_4_.refs_1_), channel_id=1, source_target_pairs={{8,16},{16,8},{9,17},{17,9},{10,18},{18,10},{11,19},{19,11},{12,20... | collective-permute-start | bytes 1474568 | tf_op jit(solution)/shard_map/ppermute | solution.py:327
  101.6 17.7 %collective-permute-start.19 = (bf16[384,640]{1,0:T(8,128)(2,1)S(1)}, bf16[384,640]{1,0:T(8,128)(2,1)S(1)}, u32[]{:S(2)}, u32[]{:S(2)}) collective-permute-start(bf16[384,640]{1,0:T(8,128)(2,1)S(1)} %get-tuple-element.63), channel_id=1, source_target_pairs={{0,8},{24,16},{8,0},{16,24},{1,9},{25,17},{9,1},{17,25},{2,10},{26... | collective-permute-start | bytes 1474568 | tf_op jit(solution)/shard_map/ppermute | solution.py:336
  107.2 13.1 %collective-permute-start.25 = (bf16[128,1280]{1,0:T(8,128)(2,1)S(1)}, bf16[128,1280]{1,0:T(8,128)(2,1)S(1)}, u32[]{:S(2)}, u32[]{:S(2)}) collective-permute-start(bf16[128,1280]{1,0:T(8,128)(2,1)S(1)} %get-tuple-element.74), channel_id=1, source_target_pairs={{0,4},{4,0},{1,5},{5,1},{2,6},{6,2},{3,7},{7,3},{8,12},{12,8},{9,1... | collective-permute-start | bytes 983048 | tf_op jit(solution)/shard_map/ppermute | solution.py:530
  112.8 16.4 %collective-permute-start.23 = (bf16[384,640]{1,0:T(8,128)(2,1)S(1)}, bf16[384,640]{1,0:T(8,128)(2,1)S(1)}, u32[]{:S(2)}, u32[]{:S(2)}) collective-permute-start(bf16[384,640]{1,0:T(8,128)(2,1)S(1)} %get-tuple-element.71), channel_id=1, source_target_pairs={{0,8},{24,16},{8,0},{16,24},{1,9},{25,17},{9,1},{17,25},{2,10},{26... | collective-permute-start | bytes 1474568 | tf_op jit(solution)/shard_map/ppermute | solution.py:336
  121.1 33.7 %collective-permute-start.26 = (bf16[128,1280]{1,0:T(8,128)(2,1)}, bf16[128,1280]{1,0:T(8,128)(2,1)}, u32[]{:S(2)}, u32[]{:S(2)}) collective-permute-start(bf16[128,1280]{1,0:T(8,128)(2,1)} %get-tuple-element.76), channel_id=1, source_target_pairs={{4,0},{0,2},{5,1},{1,3},{2,6},{6,4},{3,7},{7,5},{12,8},{8,10},{13,... | collective-permute-start | bytes 983048 | tf_op jit(solution)/shard_map/ppermute | solution.py:573
  121.3 33.5 %collective-permute-start.27 = (bf16[128,1280]{1,0:T(8,128)(2,1)}, bf16[128,1280]{1,0:T(8,128)(2,1)}, u32[]{:S(2)}, u32[]{:S(2)}) collective-permute-start(bf16[128,1280]{1,0:T(8,128)(2,1)} %get-tuple-element.78), channel_id=1, source_target_pairs={{2,4},{3,5},{4,2},{5,3},{10,12},{11,13},{12,10},{13,11},{18,20},{1... | collective-permute-start | bytes 983048 | tf_op jit(solution)/shard_map/ppermute | solution.py:574
  124.2 16.9 %collective-permute-start.29 = (bf16[384,640]{1,0:T(8,128)(2,1)}, bf16[384,640]{1,0:T(8,128)(2,1)S(1)}, u32[]{:S(2)}, u32[]{:S(2)}) collective-permute-start(bf16[384,640]{1,0:T(8,128)(2,1)} %get-tuple-element.79), channel_id=1, source_target_pairs={{0,8},{24,16},{8,0},{16,24},{1,9},{25,17},{9,1},{17,25},{2,10},{26... | collective-permute-start | bytes 1474568 | tf_op jit(solution)/shard_map/ppermute | solution.py:336
  129.4 12.7 %collective-permute-start.28 = (bf16[384,640]{1,0:T(8,128)(2,1)S(1)}, bf16[384,640]{1,0:T(8,128)(2,1)}, u32[]{:S(2)}, u32[]{:S(2)}) collective-permute-start(bf16[384,640]{1,0:T(8,128)(2,1)S(1)} %line_sum.10.refs_2_.refs_0_), channel_id=1, source_target_pairs={{8,16},{16,8},{9,17},{17,9},{10,18},{18,10},{11,19},{19,11},{12,20... | collective-permute-start | bytes 1474568 | tf_op jit(solution)/shard_map/ppermute | solution.py:327
  131.9 22.1 %collective-permute-start.32 = (bf16[384,640]{1,0:T(8,128)(2,1)S(1)}, bf16[384,640]{1,0:T(8,128)(2,1)S(1)}, u32[]{:S(2)}, u32[]{:S(2)}) collective-permute-start(bf16[384,640]{1,0:T(8,128)(2,1)S(1)} %get-tuple-element.80.refs_2_), channel_id=1, source_target_pairs={{8,0},{16,24},{9,1},{17,25},{10,2},{18,26},{11,3},{19,27},{12,4},{... | collective-permute-start | bytes 1474568 | tf_op jit(solution)/shard_map/ppermute | solution.py:341
  133.3 25.7 %all-to-all-start.1 = ((bf16[16,8,1280]{2,1,0:T(8,128)(2,1)}), bf16[16,8,1280]{2,1,0:T(8,128)(2,1)}, u32[]{:S(2)}, u32[]{:S(2)}) async-start(bf16[16,8,1280]{2,1,0:T(8,128)(2,1)} %bitcast.9), calls=%async_computation.1 | async-start | bytes 655360 | tf_op jit(solution)/shard_map/all_to_all | solution.py:561
  141.3 20.2 %collective-permute-start.31 = (bf16[384,640]{1,0:T(8,128)(2,1)S(1)}, bf16[384,640]{1,0:T(8,128)(2,1)S(1)}, u32[]{:S(2)}, u32[]{:S(2)}) collective-permute-start(bf16[384,640]{1,0:T(8,128)(2,1)S(1)} %line_sum.11.refs_2_.refs_0_), channel_id=1, source_target_pairs={{8,16},{16,8},{9,17},{17,9},{10,18},{18,10},{11,19},{19,11},{12,20... | collective-permute-start | bytes 1474568 | tf_op jit(solution)/shard_map/ppermute | solution.py:327
  143.3 21.8 %collective-permute-start.30 = (bf16[384,640]{1,0:T(8,128)(2,1)S(1)}, bf16[384,640]{1,0:T(8,128)(2,1)}, u32[]{:S(2)}, u32[]{:S(2)}) collective-permute-start(bf16[384,640]{1,0:T(8,128)(2,1)S(1)} %line_total.10.refs_8_.refs_2_), channel_id=1, source_target_pairs={{8,0},{16,24},{9,1},{17,25},{10,2},{18,26},{11,3},{19,27},{12,4},{... | collective-permute-start | bytes 1474568 | tf_op jit(solution)/shard_map/ppermute | solution.py:341
  162.6 15.9 %collective-permute-start.33 = (bf16[384,640]{1,0:T(8,128)(2,1)S(1)}, bf16[384,640]{1,0:T(8,128)(2,1)S(1)}, u32[]{:S(2)}, u32[]{:S(2)}) collective-permute-start(bf16[384,640]{1,0:T(8,128)(2,1)S(1)} %line_total.11), channel_id=1, source_target_pairs={{8,0},{16,24},{9,1},{17,25},{10,2},{18,26},{11,3},{19,27},{12,4},{... | collective-permute-start | bytes 1474568 | tf_op jit(solution)/shard_map/ppermute | solution.py:341
  (32 other events, 218.1 us)

commit v2 on v1

--- a/solution.py
+++ b/solution.py
@@ -11,7 +11,7 @@
 BLOCK = 8
 GATE_ROW = 6
 CORE, ALIGNED, LOCAL, MIDDLE = range(4)
-VMEM_BYTES = 24 * 1024 * 1024
+VMEM_BYTES = 16 * 1024 * 1024
 LINE_BYTES = 8 * 1024 * 1024
 BF = jnp.bfloat16
 F32 = jnp.float32
@@ -51,6 +51,7 @@
 
     specs = [whole(v[1].shape) if isinstance(v, tuple) else VMEM for v in operands]
     operands = [v[1] if isinstance(v, tuple) else v for v in operands]
+    after = [v[1] if isinstance(v, tuple) else v for v in after]
     got = pl.pallas_call(
         body,
         grid=(1,),
@@ -428,20 +429,6 @@
     (shared,) = call(pack_kernel, [shape((3 * hidden_s, width), BF)], [far(v) for v in weights], "pack_weights")
     shared_oth = core_swap(shared)
 
-    (send_rows,) = call(
-        functools.partial(select_kernel, n_dp),
-        [shape((slots, 2 * feat), BF)],
-        [far(v) for v in (route_expert, route_slot, gate_values, layer_input, grad_out)],
-        "select_rows",
-        after=[shared_oth],
-    )
-    back_rows = lax.all_to_all(
-        send_rows.reshape(groups, BLOCK, 2 * feat),
-        ("node", "dp"),
-        split_axis=0,
-        concat_axis=0,
-        tiled=True,
-    ).reshape(slots, 2 * feat)
 
     halves = 2 if hidden_s % 256 == 0 else 1
     part = hidden_s // halves
@@ -456,23 +443,38 @@
             name,
             [flags],
             after,
-            far_outs=(0, 1),
+            far_outs=(0, 1, 2),
         )
         sums = [got[0]]
         for step in range(1, outer):
             sums.append(lax.ppermute(got[step], "dp", outer_shift(step)))
         return x_keep, core_swap(x_send), sums
 
-    x_keep, x_recv, ab_sums = partial(x_blocks, shared, shared_oth, 0, 2, "shared_ab", [send_rows])
+    x_keep, x_recv, ab_sums = partial(x_blocks, shared, shared_oth, 0, 2, "shared_ab", [])
+    (send_rows,) = call(
+        functools.partial(select_kernel, n_dp),
+        [shape((slots, 2 * feat), BF)],
+        [far(v) for v in (route_expert, route_slot, gate_values, layer_input, grad_out)],
+        "select_rows",
+        after=ab_sums[1:2],
+        far_outs=(0,),
+    )
+    back_rows = lax.all_to_all(
+        send_rows.reshape(groups, BLOCK, 2 * feat),
+        ("node", "dp"),
+        split_axis=0,
+        concat_axis=0,
+        tiled=True,
+    ).reshape(slots, 2 * feat)
     dy_keep, dy_recv, e_sums = partial(
-        dy_blocks, shared, shared_oth, 2, 1, "shared_e", ab_sums[:1]
+        dy_blocks, shared, shared_oth, 2, 1, "shared_e", [far(ab_sums[0])]
     )
     values = call(
         functools.partial(slope_kernel, len(e_sums)),
         [shape((3 * tokens, part), BF)] * halves,
-        ab_sums + e_sums,
+        [far(v) if v.dtype == F32 else v for v in ab_sums + e_sums],
         "shared_slopes",
-        after=[x_recv, dy_recv],
+        after=[x_recv, dy_recv, far(send_rows)],
     )
     pair = n_local == 2
     swap_local = [(0, 1), (1, 0)]
@@ -496,7 +498,7 @@
 
     line = LineOfFour(flags) if n_node == 4 else None
     slopes = [gather_groups(values[0])]
-    parts = weight_grads(slopes[0], row_operands[1:])
+    parts = weight_grads(slopes[0], ())
     if line:
         line.add(parts)
         parts = line.values
@@ -521,7 +523,7 @@
             pltpu.VMEM((slots, model), BF),
             pltpu.VMEM((slots, model), BF),
         ],
-        compiler_params=pltpu.CompilerParams(vmem_limit_bytes=VMEM_BYTES),
+        compiler_params=pltpu.CompilerParams(vmem_limit_bytes=24 * 1024 * 1024),
         cost_estimate=pl.CostEstimate(flops=0, bytes_accessed=0, transcendentals=0),
         name="routed_expert",
     )(flags, *row_operands, *experts, *waits)
@@ -540,8 +542,8 @@
         else:
             parts = parts + more
     if line:
+        line.sum()
         line.sum(rows_out[:1])
-        line.sum()
         line.total()
     dx_blocks = call(
         functools.partial(shared_dx_kernel, outer, halves),
@@ -591,7 +593,7 @@
         far_outs=(0, 1),
     )
     if line:
-        line.total([grad_x])
+        line.total([far(grad_gates)])
         parts = line.finish(middle)
     else:
         depth = jnp.minimum(node, n_node - 1 - node)

time: 181 us -> 197 us (1.088)
  Pallas kernels: 36.9 us -> 46.5 us
  starting transfers between devices: 65.4 us -> 72.8 us
  waiting for transfers between devices: 60 us -> 65.3 us
  local copies, waits for them, and re-layouts: 7.76 us -> 2.6 us
    ppermute x2, waiting for transfers between devices: 5.21 us -> 19.8 us  [partial(): sums.append(lax.ppermute(got[step], 'dp', outer_shift(step)))]
    pallas_call x22, Pallas kernels: 26.4 us -> 36.1 us  [call(): pl.pallas_call(body, grid=(1,), out_shape=[pltpu.HBM(v.shape, v.dtype) if...]
    unnamed x40 -> x44, local copies, waits for them, and re-layouts: 7.76 us -> 2.6 us
    ppermute x7, waiting for transfers between devices: 6.59 us -> 1.59 us  [core_swap(): return lax.ppermute(value, 'dp', swap_core)]
    ppermute x2, waiting for transfers between devices: 1.81 us -> 6.8 us  [add(): self.outer.append(lax.ppermute(value, 'node', INWARD))]
    ppermute x2, starting transfers between devices: 2.62 us -> 6.55 us  [partial(): sums.append(lax.ppermute(got[step], 'dp', outer_shift(step)))]
    ppermute x2, waiting for transfers between devices: 10.7 us -> 7.1 us  [feature_blocks(): first = lax.ppermute(own, ('local', 'dp'), straight)]
    all_to_all x1, waiting for transfers between devices: 4.18 us -> 0.88 us  [on_device(): lax.all_to_all(row_sum.reshape(groups, BLOCK, feat), ('node', 'dp'), spli...]
  transfers between devices with their start and end apart: 36 -> 36, of which waited for: 11 -> 11; matrix products, arithmetic and copies ran while one was open for 4% -> 3% of each run, Pallas kernels for 17% -> 20%
where the time goes in v2:
time: 197 us; the launch traced here: 196 us
  starting transfers between devices  72.8 us (37%)
  waiting for transfers between devices  65.3 us (33%)
  Pallas kernels  46.5 us (24%)
  other arithmetic  7.77 us (4%)
  local copies, waits for them, and re-layouts  2.6 us (1%)
    pallas_call x22, Pallas kernels, call(): pl.pallas_call(body, grid=(1,), out_shape=[pltpu.HBM(v.shape, v.dtype) if...  36.1 us
    ppermute x3, waiting for transfers between devices, total(): came = lax.ppermute(got[0], 'node', OUTWARD)  20.6 us
    ppermute x2, waiting for transfers between devices, partial(): sums.append(lax.ppermute(got[step], 'dp', outer_shift(step)))  19.8 us
    ppermute x3, starting transfers between devices, total(): came = lax.ppermute(got[1], 'node', INWARD + OUTWARD)  12.5 us
    pallas_call x1, Pallas kernels, on_device(): pl.pallas_call(functools.partial(routed_kernel, pair, n_local, len(waits)...  10.5 us
    ppermute x1, starting transfers between devices, sum(): self.outer.append(lax.ppermute(got[1], 'node', INWARD))  7.33 us
    ppermute x2, waiting for transfers between devices, feature_blocks(): first = lax.ppermute(own, ('local', 'dp'), straight)  7.1 us
    ppermute x2, waiting for transfers between devices, gather_groups(): near.append(lax.ppermute(value, 'dp', outer_shift(outer - step)))  6.93 us
  transfers between devices with their start and end apart: 36, of which 11 were waited for; matrix products, arithmetic and copies ran while one was open for 3% of the time, Pallas kernels for 20%

profile of v2, /device:TPU:0, one launch (start us, length us, event | category | flops | bytes accessed | tf_op | source)
XLA Modules:
  0.0 196.1 jit_solution(2858908651047728316)
XLA Ops:
  3.2 2.6 %collective-permute-start = (bf16[128,1280]{1,0:T(8,128)(2,1)}, bf16[128,1280]{1,0:T(8,128)(2,1)S(1)}, u32[]{:S(2)}, u32[]{:S(2)}) collective-permute-start(bf16[128,1280]{1,0:T(8,128)(2,1)} %refs_3_.1), channel_id=1, source_target_pairs={{0,4},{2,0},{1,5},{3,1},{6,2},{4,6},{7,3},{5,7},{8,12},{10,8},{9,1... | collective-permute-start | bytes 983048 | tf_op jit(solution)/shard_map/ppermute | solution.py:408
  7.2 7.1 %collective-permute-done.refs_2_ = bf16[128,1280]{1,0:T(8,128)(2,1)S(1)} collective-permute-done((bf16[128,1280]{1,0:T(8,128)(2,1)}, bf16[128,1280]{1,0:T(8,128)(2,1)S(1)}, u32[]{:S(2)}, u32[]{:S(2)}) %collective-permute-start) | collective-permute-done | bytes 327712 | tf_op jit(solution)/shard_map/ppermute | solution.py:408
  14.3 4.4 %shared_ab.1 = (bf16[256,640]{1,0:T(8,128)(2,1)}, bf16[256,640]{1,0:T(8,128)(2,1)}, f32[256,768]{1,0:T(8,128)}, bf16[256,768]{1,0:T(8,128)(2,1)S(1)}) custom-call(s32[4]{0:T(128)S(1)} %pad_add_fusion.refs_0_.flag_ref, bf16[128,1280]{1,0:T(8,128)(2,1)} %refs_3_.1, bf16[128,1280]{1,0:T(8,128)(2,1)S(1)} %collective-permute-done.refs_2_, ...), custom_call_target="tpu_custom_call" | custom-call | tf_op jit(solution)/shard_map/shared_ab/pallas_call | solution.py:55
  18.7 4.7 %collective-permute-start.7 = (bf16[256,768]{1,0:T(8,128)(2,1)S(1)}, bf16[256,768]{1,0:T(8,128)(2,1)S(1)}, u32[]{:S(2)}, u32[]{:S(2)}) collective-permute-start(bf16[256,768]{1,0:T(8,128)(2,1)S(1)} %get-tuple-element.52), channel_id=1, source_target_pairs={{0,2},{1,3},{2,0},{3,1},{4,6},{5,7},{6,4},{7,5},{8,10},{9,11},{10,... | collective-permute-start | bytes 1179656 | tf_op jit(solution)/shard_map/ppermute | solution.py:450
  25.9 12.7 %collective-permute-done.7.refs_5_.refs_1_ = bf16[256,768]{1,0:T(8,128)(2,1)S(1)} collective-permute-done((bf16[256,768]{1,0:T(8,128)(2,1)S(1)}, bf16[256,768]{1,0:T(8,128)(2,1)S(1)}, u32[]{:S(2)}, u32[]{:S(2)}) %collective-permute-start.7) | collective-permute-done | bytes 393248 | tf_op jit(solution)/shard_map/ppermute | solution.py:450
  41.6 6.8 %all-to-all-start = ((bf16[16,8,2560]{2,1,0:T(8,128)(2,1)}), bf16[16,8,2560]{2,1,0:T(8,128)(2,1)}, u32[]{:S(2)}, u32[]{:S(2)}) async-start(bf16[16,8,2560]{2,1,0:T(8,128)(2,1)} %bitcast.12), calls=%async_computation | async-start | bytes 1310720 | tf_op jit(solution)/shard_map/all_to_all | solution.py:462
  48.4 3.7 %shared_e.1 = (bf16[256,640]{1,0:T(8,128)(2,1)}, bf16[256,640]{1,0:T(8,128)(2,1)}, f32[128,768]{1,0:T(8,128)}, bf16[128,768]{1,0:T(8,128)(2,1)S(1)}) custom-call(s32[4]{0:T(128)S(1)} %pad_add_fusion.refs_0_.flag_ref, bf16[128,1280]{1,0:T(8,128)(2,1)} %refs_4_.1, bf16[128,1280]{1,0:T(8,128)(2,1)S(1)} %collective-permute-done.4.refs_2_, ...), custom_call_target="tpu_custom_call" | custom-call | tf_op jit(solution)/shard_map/shared_e/pallas_call | solution.py:55
  54.5 7.2 %collective-permute-done.8.refs_3_ = bf16[128,768]{1,0:T(8,128)(2,1)S(1)} collective-permute-done((bf16[128,768]{1,0:T(8,128)(2,1)S(1)}, bf16[128,768]{1,0:T(8,128)(2,1)S(1)}, u32[]{:S(2)}, u32[]{:S(2)}) %collective-permute-start.8) | collective-permute-done | bytes 196640 | tf_op jit(solution)/shard_map/ppermute | solution.py:450
  64.0 2.5 %collective-permute-start.9 = (bf16[384,384]{1,0:T(8,128)(2,1)S(1)}, bf16[384,384]{1,0:T(8,128)(2,1)S(1)}, u32[]{:S(2)}, u32[]{:S(2)}) collective-permute-start(bf16[384,384]{1,0:T(8,128)(2,1)S(1)} %get-tuple-element.55.refs_4_.refs_1_), channel_id=1, source_target_pairs={{0,2},{1,3},{2,0},{3,1},{4,6},{5,7},{6,4},{7,5},{8,10},{9,11},{10,... | collective-permute-start | bytes 884744 | tf_op jit(solution)/shard_map/ppermute | solution.py:422
  66.5 6.9 %collective-permute-done.9.refs_0_.refs_5_.refs_2_ = bf16[384,384]{1,0:T(8,128)(2,1)S(1)} collective-permute-done((bf16[384,384]{1,0:T(8,128)(2,1)S(1)}, bf16[384,384]{1,0:T(8,128)(2,1)S(1)}, u32[]{:S(2)}, u32[]{:S(2)}) %collective-permute-start.9) | collective-permute-done | bytes 294944 | tf_op jit(solution)/shard_map/ppermute | solution.py:422
  75.0 3.2 %shared_weight_grads.2 = (bf16[384,640]{1,0:T(8,128)(2,1)}, bf16[384,640]{1,0:T(8,128)(2,1)S(1)}, bf16[384,640]{1,0:T(8,128)(2,1)}) custom-call(bf16[256,640]{1,0:T(8,128)(2,1)} %get-tuple-element.47.refs_0_, bf16[256,640]{1,0:T(8,128)(2,1)} %copy-done.2, bf16[256,640]{1,0:T(8,128)(2,1)} %get-tuple-element.50.refs_2_, bf16[256,640]{1,0:T(8,128)(2,1)} %copy-done.1, ...), custom_call_target="tpu_custom_call" | custom-call | tf_op jit(solution)/shard_map/shared_weight_grads/pallas_call | solution.py:55
  79.0 4.3 %collective-permute-start.16 = (bf16[384,640]{1,0:T(8,128)(2,1)}, bf16[384,640]{1,0:T(8,128)(2,1)S(1)}, u32[]{:S(2)}, u32[]{:S(2)}) collective-permute-start(bf16[384,640]{1,0:T(8,128)(2,1)} %get-tuple-element.57.refs_0_), channel_id=1, source_target_pairs={{0,8},{24,16},{1,9},{25,17},{2,10},{26,18},{3,11},{27,19},{4,12},{... | collective-permute-start | bytes 1474568 | tf_op jit(solution)/shard_map/ppermute | solution.py:312
  88.4 6.8 %collective-permute-done.16.refs_1_ = bf16[384,640]{1,0:T(8,128)(2,1)S(1)} collective-permute-done((bf16[384,640]{1,0:T(8,128)(2,1)}, bf16[384,640]{1,0:T(8,128)(2,1)S(1)}, u32[]{:S(2)}, u32[]{:S(2)}) %collective-permute-start.16) | collective-permute-done | bytes 491552 | tf_op jit(solution)/shard_map/ppermute | solution.py:312
  97.1 7.3 %collective-permute-start.21 = (bf16[384,640]{1,0:T(8,128)(2,1)}, bf16[384,640]{1,0:T(8,128)(2,1)S(1)}, u32[]{:S(2)}, u32[]{:S(2)}) collective-permute-start(bf16[384,640]{1,0:T(8,128)(2,1)} %get-tuple-element.65.refs_0_), channel_id=1, source_target_pairs={{0,8},{24,16},{1,9},{25,17},{2,10},{26,18},{3,11},{27,19},{4,12},{... | collective-permute-start | bytes 1474568 | tf_op jit(solution)/shard_map/ppermute | solution.py:326
  105.0 10.5 %routed_expert.1 = (bf16[1,384,2560]{2,1,0:T(8,128)(2,1)}, bf16[1,384,2560]{2,1,0:T(8,128)(2,1)}, bf16[1,384,2560]{2,1,0:T(8,128)(2,1)}, bf16[128,1280]{1,0:T(8,128)(2,1)S(1)}, bf16[128,1280]{1,0:T(8,128)(2,1)S(1)}) custom-call(s32[4]{0:T(128)S(1)} %pad_add_fusion.refs_0_.flag_ref, bf16[128,2560]{1,0:T(8,128)(2,1)} %bitcast.8.x_ref, ...), custom_call_target="tpu_custom_call" | custom-call | tf_op jit(solution)/shard_map/routed_expert/pallas_call | solution.py:511
  116.5 2.5 %shared_weight_grads.3 = (bf16[384,640]{1,0:T(8,128)(2,1)S(1)}, bf16[384,640]{1,0:T(8,128)(2,1)S(1)}, bf16[384,640]{1,0:T(8,128)(2,1)S(1)}) custom-call(bf16[256,640]{1,0:T(8,128)(2,1)} %get-tuple-element.47.refs_0_, bf16[256,640]{1,0:T(8,128)(2,1)} %copy-done.2, bf16[256,640]{1,0:T(8,128)(2,1)} %get-tuple-element.50.refs_2_, bf16[256,640]{1,0:T(8,128)(2,1)} %copy-done.1, ...), custom_call_target="tpu_custom_call" | custom-call | tf_op jit(solution)/shard_map/shared_weight_grads/pallas_call | solution.py:55
  120.7 4.2 %shared_dx.1 = (bf16[128,1280]{1,0:T(8,128)(2,1)S(1)}, bf16[128,1280]{1,0:T(8,128)(2,1)}, bf16[128,1280]{1,0:T(8,128)(2,1)}) custom-call(s32[4]{0:T(128)S(1)} %pad_add_fusion.refs_0_.flag_ref, bf16[384,384]{1,0:T(8,128)(2,1)S(1)} %copy-done.15, bf16[384,384]{1,0:T(8,128)(2,1)S(1)} %copy-done.5, bf16[384,384]{1,0:T(8,128)(2,1)} %hold.1.refs_4_.refs_3_, ...), custom_call_target="tpu_custom_call" | custom-call | tf_op jit(solution)/shard_map/shared_dx/pallas_call | solution.py:55
  129.2 3.0 %collective-permute-start.23 = (bf16[384,640]{1,0:T(8,128)(2,1)S(1)}, bf16[384,640]{1,0:T(8,128)(2,1)S(1)}, u32[]{:S(2)}, u32[]{:S(2)}) collective-permute-start(bf16[384,640]{1,0:T(8,128)(2,1)S(1)} %get-tuple-element.71), channel_id=1, source_target_pairs={{0,8},{24,16},{8,0},{16,24},{1,9},{25,17},{9,1},{17,25},{2,10},{26... | collective-permute-start | bytes 1474568 | tf_op jit(solution)/shard_map/ppermute | solution.py:337
  136.2 8.5 %collective-permute-start.29 = (bf16[384,640]{1,0:T(8,128)(2,1)}, bf16[384,640]{1,0:T(8,128)(2,1)S(1)}, u32[]{:S(2)}, u32[]{:S(2)}) collective-permute-start(bf16[384,640]{1,0:T(8,128)(2,1)} %get-tuple-element.79), channel_id=1, source_target_pairs={{0,8},{24,16},{8,0},{16,24},{1,9},{25,17},{9,1},{17,25},{2,10},{26... | collective-permute-start | bytes 1474568 | tf_op jit(solution)/shard_map/ppermute | solution.py:337
  153.5 5.8 %all-to-all-start.1 = ((bf16[16,8,1280]{2,1,0:T(8,128)(2,1)}), bf16[16,8,1280]{2,1,0:T(8,128)(2,1)}, u32[]{:S(2)}, u32[]{:S(2)}) async-start(bf16[16,8,1280]{2,1,0:T(8,128)(2,1)} %bitcast.9), calls=%async_computation.1 | async-start | bytes 655360 | tf_op jit(solution)/shard_map/all_to_all | solution.py:563
  164.4 5.7 %collective-permute-done.32.refs_4_ = bf16[384,640]{1,0:T(8,128)(2,1)S(1)} collective-permute-done((bf16[384,640]{1,0:T(8,128)(2,1)}, bf16[384,640]{1,0:T(8,128)(2,1)S(1)}, u32[]{:S(2)}, u32[]{:S(2)}) %collective-permute-start.32) | collective-permute-done | bytes 491552 | tf_op jit(solution)/shard_map/ppermute | solution.py:342
  171.9 2.5 %combine.1 = (bf16[128,1280]{1,0:T(8,128)(2,1)}, f32[6,128]{1,0:T(8,128)}) custom-call(s32[4]{0:T(128)S(1)} %pad_add_fusion.refs_0_.flag_ref, s32[6,128]{1,0:T(8,128)} %bitcast.14, s32[6,128]{1,0:T(8,128)} %bitcast.16, bf16[6,128]{1,0:T(8,128)(2,1)} %bitcast.18, bf16[128,1280]{1,0:T(8,128)(2,1)} %bitcast.10.refs_4_, ...), custom_call_target="tpu_custom_call" | custom-call | tf_op jit(solution)/shard_map/combine/pallas_call | solution.py:55
  177.9 3.4 %collective-permute-done.30 = bf16[384,640]{1,0:T(8,128)(2,1)} collective-permute-done((bf16[384,640]{1,0:T(8,128)(2,1)S(1)}, bf16[384,640]{1,0:T(8,128)(2,1)}, u32[]{:S(2)}, u32[]{:S(2)}) %collective-permute-start.30) | collective-permute-done | bytes 491552 | tf_op jit(solution)/shard_map/ppermute | solution.py:342
  183.4 11.6 %collective-permute-done.33 = bf16[384,640]{1,0:T(8,128)(2,1)S(1)} collective-permute-done((bf16[384,640]{1,0:T(8,128)(2,1)S(1)}, bf16[384,640]{1,0:T(8,128)(2,1)S(1)}, u32[]{:S(2)}, u32[]{:S(2)}) %collective-permute-start.33) | collective-permute-done | bytes 491552 | tf_op jit(solution)/shard_map/ppermute | solution.py:342
  (126 shorter events, 57.4 us)
Async XLA Ops:
  18.7 19.9 %collective-permute-start.7 = (bf16[256,768]{1,0:T(8,128)(2,1)S(1)}, bf16[256,768]{1,0:T(8,128)(2,1)S(1)}, u32[]{:S(2)}, u32[]{:S(2)}) collective-permute-start(bf16[256,768]{1,0:T(8,128)(2,1)S(1)} %get-tuple-element.52), channel_id=1, source_target_pairs={{0,2},{1,3},{2,0},{3,1},{4,6},{5,7},{6,4},{7,5},{8,10},{9,11},{10,... | collective-permute-start | bytes 1179656 | tf_op jit(solution)/shard_map/ppermute | solution.py:450
  23.3 25.1 %collective-permute-start.4 = (bf16[128,1280]{1,0:T(8,128)(2,1)}, bf16[128,1280]{1,0:T(8,128)(2,1)S(1)}, u32[]{:S(2)}, u32[]{:S(2)}) collective-permute-start(bf16[128,1280]{1,0:T(8,128)(2,1)} %refs_4_.1), channel_id=1, source_target_pairs={{0,4},{2,0},{1,5},{3,1},{6,2},{4,6},{7,3},{5,7},{8,12},{10,8},{9,1... | collective-permute-start | bytes 983048 | tf_op jit(solution)/shard_map/ppermute | solution.py:408
  24.5 23.9 %collective-permute-start.5 = (bf16[128,1280]{1,0:T(8,128)(2,1)}, bf16[128,1280]{1,0:T(8,128)(2,1)}, u32[]{:S(2)}, u32[]{:S(2)}) collective-permute-start(bf16[128,1280]{1,0:T(8,128)(2,1)} %refs_4_.1), channel_id=1, source_target_pairs={{2,4},{3,5},{4,2},{5,3},{10,12},{11,13},{12,10},{13,11},{18,20},{1... | collective-permute-start | bytes 983048 | tf_op jit(solution)/shard_map/ppermute | solution.py:409
  41.6 41.8 %all-to-all-start = ((bf16[16,8,2560]{2,1,0:T(8,128)(2,1)}), bf16[16,8,2560]{2,1,0:T(8,128)(2,1)}, u32[]{:S(2)}, u32[]{:S(2)}) async-start(bf16[16,8,2560]{2,1,0:T(8,128)(2,1)} %bitcast.12), calls=%async_computation | async-start | bytes 1310720 | tf_op jit(solution)/shard_map/all_to_all | solution.py:462
  79.0 16.2 %collective-permute-start.16 = (bf16[384,640]{1,0:T(8,128)(2,1)}, bf16[384,640]{1,0:T(8,128)(2,1)S(1)}, u32[]{:S(2)}, u32[]{:S(2)}) collective-permute-start(bf16[384,640]{1,0:T(8,128)(2,1)} %get-tuple-element.57.refs_0_), channel_id=1, source_target_pairs={{0,8},{24,16},{1,9},{25,17},{2,10},{26,18},{3,11},{27,19},{4,12},{... | collective-permute-start | bytes 1474568 | tf_op jit(solution)/shard_map/ppermute | solution.py:312
  83.4 21.1 %collective-permute-start.13 = (bf16[128,2560]{1,0:T(8,128)(2,1)}, bf16[128,2560]{1,0:T(8,128)(2,1)S(1)}, u32[]{:S(2)}, u32[]{:S(2)}) collective-permute-start(bf16[128,2560]{1,0:T(8,128)(2,1)} %bitcast.8.x_ref), channel_id=1, source_target_pairs={{0,4},{4,0},{1,5},{5,1},{2,6},{6,2},{3,7},{7,3},{8,12},{12,8},{9,1... | collective-permute-start | bytes 1966088 | tf_op jit(solution)/shard_map/ppermute | solution.py:482
  85.9 18.5 %collective-permute-start.10 = (bf16[384,384]{1,0:T(8,128)(2,1)}, bf16[384,384]{1,0:T(8,128)(2,1)S(1)}, u32[]{:S(2)}, u32[]{:S(2)}) collective-permute-start(bf16[384,384]{1,0:T(8,128)(2,1)} %hold.1.refs_4_.refs_3_), channel_id=1, source_target_pairs={{0,2},{1,3},{2,0},{3,1},{4,6},{5,7},{6,4},{7,5},{8,10},{9,11},{10,... | collective-permute-start | bytes 884744 | tf_op jit(solution)/shard_map/ppermute | solution.py:422
  87.1 28.4 %collective-permute-start.18 = (bf16[384,640]{1,0:T(8,128)(2,1)}, bf16[384,640]{1,0:T(8,128)(2,1)S(1)}, u32[]{:S(2)}, u32[]{:S(2)}) collective-permute-start(bf16[384,640]{1,0:T(8,128)(2,1)} %copy-done.16), channel_id=1, source_target_pairs={{0,8},{24,16},{1,9},{25,17},{2,10},{26,18},{3,11},{27,19},{4,12},{... | collective-permute-start | bytes 1474568 | tf_op jit(solution)/shard_map/ppermute | solution.py:312
  96.4 22.6 %collective-permute-start.17 = (bf16[384,640]{1,0:T(8,128)(2,1)S(1)}, bf16[384,640]{1,0:T(8,128)(2,1)S(1)}, u32[]{:S(2)}, u32[]{:S(2)}) collective-permute-start(bf16[384,640]{1,0:T(8,128)(2,1)S(1)} %get-tuple-element.61.refs_2_.refs_1_), channel_id=1, source_target_pairs={{8,16},{16,8},{9,17},{17,9},{10,18},{18,10},{11,19},{19,11},{12,20... | collective-permute-start | bytes 1474568 | tf_op jit(solution)/shard_map/ppermute | solution.py:328
  97.1 27.9 %collective-permute-start.21 = (bf16[384,640]{1,0:T(8,128)(2,1)}, bf16[384,640]{1,0:T(8,128)(2,1)S(1)}, u32[]{:S(2)}, u32[]{:S(2)}) collective-permute-start(bf16[384,640]{1,0:T(8,128)(2,1)} %get-tuple-element.65.refs_0_), channel_id=1, source_target_pairs={{0,8},{24,16},{1,9},{25,17},{2,10},{26,18},{3,11},{27,19},{4,12},{... | collective-permute-start | bytes 1474568 | tf_op jit(solution)/shard_map/ppermute | solution.py:326
  115.6 12.8 %collective-permute-start.20 = (bf16[384,640]{1,0:T(8,128)(2,1)S(1)}, bf16[384,640]{1,0:T(8,128)(2,1)S(1)}, u32[]{:S(2)}, u32[]{:S(2)}) collective-permute-start(bf16[384,640]{1,0:T(8,128)(2,1)S(1)} %line_sum.7.refs_4_.refs_1_), channel_id=1, source_target_pairs={{8,16},{16,8},{9,17},{17,9},{10,18},{18,10},{11,19},{19,11},{12,20... | collective-permute-start | bytes 1474568 | tf_op jit(solution)/shard_map/ppermute | solution.py:328
  119.7 13.9 %collective-permute-start.19 = (bf16[384,640]{1,0:T(8,128)(2,1)S(1)}, bf16[384,640]{1,0:T(8,128)(2,1)S(1)}, u32[]{:S(2)}, u32[]{:S(2)}) collective-permute-start(bf16[384,640]{1,0:T(8,128)(2,1)S(1)} %get-tuple-element.63), channel_id=1, source_target_pairs={{0,8},{24,16},{8,0},{16,24},{1,9},{25,17},{9,1},{17,25},{2,10},{26... | collective-permute-start | bytes 1474568 | tf_op jit(solution)/shard_map/ppermute | solution.py:337
  126.8 17.9 %collective-permute-start.25 = (bf16[128,1280]{1,0:T(8,128)(2,1)S(1)}, bf16[128,1280]{1,0:T(8,128)(2,1)S(1)}, u32[]{:S(2)}, u32[]{:S(2)}) collective-permute-start(bf16[128,1280]{1,0:T(8,128)(2,1)S(1)} %get-tuple-element.74), channel_id=1, source_target_pairs={{0,4},{4,0},{1,5},{5,1},{2,6},{6,2},{3,7},{7,3},{8,12},{12,8},{9,1... | collective-permute-start | bytes 983048 | tf_op jit(solution)/shard_map/ppermute | solution.py:532
  129.2 19.5 %collective-permute-start.23 = (bf16[384,640]{1,0:T(8,128)(2,1)S(1)}, bf16[384,640]{1,0:T(8,128)(2,1)S(1)}, u32[]{:S(2)}, u32[]{:S(2)}) collective-permute-start(bf16[384,640]{1,0:T(8,128)(2,1)S(1)} %get-tuple-element.71), channel_id=1, source_target_pairs={{0,8},{24,16},{8,0},{16,24},{1,9},{25,17},{9,1},{17,25},{2,10},{26... | collective-permute-start | bytes 1474568 | tf_op jit(solution)/shard_map/ppermute | solution.py:337
  133.8 17.5 %collective-permute-start.22 = (bf16[384,640]{1,0:T(8,128)(2,1)S(1)}, bf16[384,640]{1,0:T(8,128)(2,1)S(1)}, u32[]{:S(2)}, u32[]{:S(2)}) collective-permute-start(bf16[384,640]{1,0:T(8,128)(2,1)S(1)} %line_sum.9.refs_4_.refs_0_), channel_id=1, source_target_pairs={{8,16},{16,8},{9,17},{17,9},{10,18},{18,10},{11,19},{19,11},{12,20... | collective-permute-start | bytes 1474568 | tf_op jit(solution)/shard_map/ppermute | solution.py:328
  136.2 23.1 %collective-permute-start.29 = (bf16[384,640]{1,0:T(8,128)(2,1)}, bf16[384,640]{1,0:T(8,128)(2,1)S(1)}, u32[]{:S(2)}, u32[]{:S(2)}) collective-permute-start(bf16[384,640]{1,0:T(8,128)(2,1)} %get-tuple-element.79), channel_id=1, source_target_pairs={{0,8},{24,16},{8,0},{16,24},{1,9},{25,17},{9,1},{17,25},{2,10},{26... | collective-permute-start | bytes 1474568 | tf_op jit(solution)/shard_map/ppermute | solution.py:337
  145.5 25.4 %collective-permute-start.26 = (bf16[128,1280]{1,0:T(8,128)(2,1)}, bf16[128,1280]{1,0:T(8,128)(2,1)}, u32[]{:S(2)}, u32[]{:S(2)}) collective-permute-start(bf16[128,1280]{1,0:T(8,128)(2,1)} %get-tuple-element.76), channel_id=1, source_target_pairs={{4,0},{0,2},{5,1},{1,3},{2,6},{6,4},{3,7},{7,5},{12,8},{8,10},{13,... | collective-permute-start | bytes 983048 | tf_op jit(solution)/shard_map/ppermute | solution.py:575
  147.3 23.7 %collective-permute-start.27 = (bf16[128,1280]{1,0:T(8,128)(2,1)}, bf16[128,1280]{1,0:T(8,128)(2,1)}, u32[]{:S(2)}, u32[]{:S(2)}) collective-permute-start(bf16[128,1280]{1,0:T(8,128)(2,1)} %get-tuple-element.78), channel_id=1, source_target_pairs={{2,4},{3,5},{4,2},{5,3},{10,12},{11,13},{12,10},{13,11},{18,20},{1... | collective-permute-start | bytes 983048 | tf_op jit(solution)/shard_map/ppermute | solution.py:576
  148.8 13.0 %collective-permute-start.28 = (bf16[384,640]{1,0:T(8,128)(2,1)S(1)}, bf16[384,640]{1,0:T(8,128)(2,1)}, u32[]{:S(2)}, u32[]{:S(2)}) collective-permute-start(bf16[384,640]{1,0:T(8,128)(2,1)S(1)} %line_sum.10.refs_2_.refs_0_), channel_id=1, source_target_pairs={{8,16},{16,8},{9,17},{17,9},{10,18},{18,10},{11,19},{19,11},{12,20... | collective-permute-start | bytes 1474568 | tf_op jit(solution)/shard_map/ppermute | solution.py:328
  152.2 17.9 %collective-permute-start.32 = (bf16[384,640]{1,0:T(8,128)(2,1)}, bf16[384,640]{1,0:T(8,128)(2,1)S(1)}, u32[]{:S(2)}, u32[]{:S(2)}) collective-permute-start(bf16[384,640]{1,0:T(8,128)(2,1)} %get-tuple-element.80.refs_2_), channel_id=1, source_target_pairs={{8,0},{16,24},{9,1},{17,25},{10,2},{18,26},{11,3},{19,27},{12,4},{... | collective-permute-start | bytes 1474568 | tf_op jit(solution)/shard_map/ppermute | solution.py:342
  153.5 18.4 %all-to-all-start.1 = ((bf16[16,8,1280]{2,1,0:T(8,128)(2,1)}), bf16[16,8,1280]{2,1,0:T(8,128)(2,1)}, u32[]{:S(2)}, u32[]{:S(2)}) async-start(bf16[16,8,1280]{2,1,0:T(8,128)(2,1)} %bitcast.9), calls=%async_computation.1 | async-start | bytes 655360 | tf_op jit(solution)/shard_map/all_to_all | solution.py:563
  159.5 14.9 %collective-permute-start.31 = (bf16[384,640]{1,0:T(8,128)(2,1)S(1)}, bf16[384,640]{1,0:T(8,128)(2,1)}, u32[]{:S(2)}, u32[]{:S(2)}) collective-permute-start(bf16[384,640]{1,0:T(8,128)(2,1)S(1)} %line_sum.11.refs_2_.refs_0_), channel_id=1, source_target_pairs={{8,16},{16,8},{9,17},{17,9},{10,18},{18,10},{11,19},{19,11},{12,20... | collective-permute-start | bytes 1474568 | tf_op jit(solution)/shard_map/ppermute | solution.py:328
  163.1 18.2 %collective-permute-start.30 = (bf16[384,640]{1,0:T(8,128)(2,1)S(1)}, bf16[384,640]{1,0:T(8,128)(2,1)}, u32[]{:S(2)}, u32[]{:S(2)}) collective-permute-start(bf16[384,640]{1,0:T(8,128)(2,1)S(1)} %line_total.10.refs_8_.refs_2_), channel_id=1, source_target_pairs={{8,0},{16,24},{9,1},{17,25},{10,2},{18,26},{11,3},{19,27},{12,4},{... | collective-permute-start | bytes 1474568 | tf_op jit(solution)/shard_map/ppermute | solution.py:342
  175.5 19.4 %collective-permute-start.33 = (bf16[384,640]{1,0:T(8,128)(2,1)S(1)}, bf16[384,640]{1,0:T(8,128)(2,1)S(1)}, u32[]{:S(2)}, u32[]{:S(2)}) collective-permute-start(bf16[384,640]{1,0:T(8,128)(2,1)S(1)} %line_total.11), channel_id=1, source_target_pairs={{8,0},{16,24},{9,1},{17,25},{10,2},{18,26},{11,3},{19,27},{12,4},{... | collective-permute-start | bytes 1474568 | tf_op jit(solution)/shard_map/ppermute | solution.py:342
  (34 other events, 295.8 us)

commit v3 on v2

--- a/solution.py
+++ b/solution.py
@@ -450,13 +450,12 @@
             sums.append(lax.ppermute(got[step], "dp", outer_shift(step)))
         return x_keep, core_swap(x_send), sums
 
-    x_keep, x_recv, ab_sums = partial(x_blocks, shared, shared_oth, 0, 2, "shared_ab", [])
     (send_rows,) = call(
         functools.partial(select_kernel, n_dp),
         [shape((slots, 2 * feat), BF)],
         [far(v) for v in (route_expert, route_slot, gate_values, layer_input, grad_out)],
         "select_rows",
-        after=ab_sums[1:2],
+        after=[shared],
         far_outs=(0,),
     )
     back_rows = lax.all_to_all(
@@ -466,6 +465,8 @@
         concat_axis=0,
         tiled=True,
     ).reshape(slots, 2 * feat)
+
+    x_keep, x_recv, ab_sums = partial(x_blocks, shared, shared_oth, 0, 2, "shared_ab", [far(send_rows)])
     dy_keep, dy_recv, e_sums = partial(
         dy_blocks, shared, shared_oth, 2, 1, "shared_e", [far(ab_sums[0])]
     )
@@ -474,7 +475,7 @@
         [shape((3 * tokens, part), BF)] * halves,
         [far(v) if v.dtype == F32 else v for v in ab_sums + e_sums],
         "shared_slopes",
-        after=[x_recv, dy_recv, far(send_rows)],
+        after=[x_recv, dy_recv],
     )
     pair = n_local == 2
     swap_local = [(0, 1), (1, 0)]
@@ -503,8 +504,19 @@
         line.add(parts)
         parts = line.values
 
+    for value in values[1:]:
+        (value,) = call(lambda: None, [], [], "hold", after=slopes[-1][1:outer], held=[value])
+        slopes.append(gather_groups(value))
+        more = weight_grads(slopes[-1], ())
+        if line:
+            line.add(more)
+        else:
+            parts = parts + more
+    if line:
+        line.sum(parts[-1:])
+
     row_outs = [shape((slots, feat), BF)] * 2 if pair else [shape((slots, model), BF)]
-    waits = parts[:1]
+    waits = parts[-1:] + (line.last if line else [])
     block = hidden_r // 2 if hidden_r % 128 == 0 else hidden_r
     tile = pl.BlockSpec((1, block, model), lambda i: (0, i, 0))
     experts = [far(v)[1] for v in (expert_gate, expert_up, expert_down)]
@@ -533,16 +545,7 @@
         row_sum = (mine.astype(F32) + came.astype(F32)).astype(BF)
     else:
         row_sum = lax.psum_scatter(rows_out[0], "local", scatter_dimension=1, tiled=True)
-    for value in values[1:]:
-        (value,) = call(lambda: None, [], [], "hold", after=slopes[-1][1:outer], held=[value])
-        slopes.append(gather_groups(value))
-        more = weight_grads(slopes[-1], rows_out[:1])
-        if line:
-            line.add(more)
-        else:
-            parts = parts + more
     if line:
-        line.sum()
         line.sum(rows_out[:1])
         line.total()
     dx_blocks = call(

time: 197 us -> 176 us (0.89)
  waiting for transfers between devices: 65.3 us -> 43 us
  Pallas kernels: 46.5 us -> 43.5 us
  local copies, waits for them, and re-layouts: 2.6 us -> 4.98 us
  starting transfers between devices: 72.8 us -> 74.9 us
    ppermute x2, waiting for transfers between devices: 19.8 us -> 10.7 us  [partial(): sums.append(lax.ppermute(got[step], 'dp', outer_shift(step)))]
    ppermute x2, waiting for transfers between devices: 6.8 us -> 0.29 us  [add(): self.outer.append(lax.ppermute(value, 'node', INWARD))]
    ppermute x2, waiting for transfers between devices: 7.1 us -> 1.69 us  [feature_blocks(): first = lax.ppermute(own, ('local', 'dp'), straight)]
    all_to_all x1, starting transfers between devices: 5.83 us -> 9.11 us  [on_device(): lax.all_to_all(row_sum.reshape(groups, BLOCK, feat), ('node', 'dp'), spli...]
    pallas_call x22, Pallas kernels: 36.1 us -> 33 us  [call(): pl.pallas_call(body, grid=(1,), out_shape=[pltpu.HBM(v.shape, v.dtype) if...]
    unnamed x44 -> x38, local copies, waits for them, and re-layouts: 2.6 us -> 4.98 us
  transfers between devices with their start and end apart: 36 -> 36, of which waited for: 11 -> 9; matrix products, arithmetic and copies ran while one was open for 3% -> 4% of each run, Pallas kernels for 20% -> 24%
where the time goes in v3:
time: 176 us; the launch traced here: 175 us
  starting transfers between devices  74.9 us (43%)
  Pallas kernels  43.5 us (25%)
  waiting for transfers between devices  43 us (24%)
  other arithmetic  7.7 us (4%)
  local copies, waits for them, and re-layouts  4.98 us (3%)
    pallas_call x22, Pallas kernels, call(): pl.pallas_call(body, grid=(1,), out_shape=[pltpu.HBM(v.shape, v.dtype) if...  33 us
    ppermute x3, waiting for transfers between devices, total(): came = lax.ppermute(got[0], 'node', OUTWARD)  20.7 us
    ppermute x3, starting transfers between devices, total(): came = lax.ppermute(got[1], 'node', INWARD + OUTWARD)  12.2 us
    ppermute x2, waiting for transfers between devices, partial(): sums.append(lax.ppermute(got[step], 'dp', outer_shift(step)))  10.7 us
    pallas_call x1, Pallas kernels, on_device(): pl.pallas_call(functools.partial(routed_kernel, pair, n_local, len(waits)...  10.5 us
    all_to_all x1, starting transfers between devices, on_device(): lax.all_to_all(row_sum.reshape(groups, BLOCK, feat), ('node', 'dp'), spli...  9.11 us
    ppermute x2, waiting for transfers between devices, gather_groups(): near.append(lax.ppermute(value, 'dp', outer_shift(outer - step)))  7.55 us
    ppermute x1, starting transfers between devices, sum(): self.outer.append(lax.ppermute(got[1], 'node', INWARD))  7.26 us
  transfers between devices with their start and end apart: 36, of which 9 were waited for; matrix products, arithmetic and copies ran while one was open for 4% of the time, Pallas kernels for 24%

profile of v3, /device:TPU:0, one launch (start us, length us, event | category | flops | bytes accessed | tf_op | source)
XLA Modules:
  0.0 175.1 jit_solution(15934744411076368836)
XLA Ops:
  3.2 2.6 %collective-permute-start = (bf16[128,1280]{1,0:T(8,128)(2,1)}, bf16[128,1280]{1,0:T(8,128)(2,1)}, u32[]{:S(2)}, u32[]{:S(2)}) collective-permute-start(bf16[128,1280]{1,0:T(8,128)(2,1)} %refs_1_.4), channel_id=1, source_target_pairs={{0,4},{2,0},{1,5},{3,1},{6,2},{4,6},{7,3},{5,7},{8,12},{10,8},{9,1... | collective-permute-start | bytes 983048 | tf_op jit(solution)/shard_map/ppermute | solution.py:408
  7.1 2.1 %collective-permute-start.4 = (bf16[128,1280]{1,0:T(8,128)(2,1)}, bf16[128,1280]{1,0:T(8,128)(2,1)S(1)}, u32[]{:S(2)}, u32[]{:S(2)}) collective-permute-start(bf16[128,1280]{1,0:T(8,128)(2,1)} %refs_1_.5), channel_id=1, source_target_pairs={{0,4},{2,0},{1,5},{3,1},{6,2},{4,6},{7,3},{5,7},{8,12},{10,8},{9,1... | collective-permute-start | bytes 983048 | tf_op jit(solution)/shard_map/ppermute | solution.py:408
  10.6 2.3 %select_rows.1.refs_6_ = bf16[128,2560]{1,0:T(8,128)(2,1)} custom-call(s32[6,128]{1,0:T(8,128)} %bitcast.13, s32[6,128]{1,0:T(8,128)} %bitcast.15, bf16[6,128]{1,0:T(8,128)(2,1)} %bitcast.17, bf16[128,1280]{1,0:T(8,128)(2,1)} %refs_1_.4, bf16[128,1280]{1,0:T(8,128)(2,1)} %refs_1_.5, bf16[2304,640]{1,0:T(8,128)(2,1)S(1)} %pack_weights.1.refs_5_.refs_4_), custom_call_target="tpu_custom_call" | custom-call | tf_op jit(solution)/shard_map/select_rows/pallas_call | solution.py:55
  14.6 4.6 %shared_ab.1 = (bf16[256,640]{1,0:T(8,128)(2,1)}, bf16[256,640]{1,0:T(8,128)(2,1)}, f32[256,768]{1,0:T(8,128)}, bf16[256,768]{1,0:T(8,128)(2,1)}) custom-call(s32[4]{0:T(128)S(1)} %pad_add_fusion.refs_0_.flag_ref, bf16[128,1280]{1,0:T(8,128)(2,1)} %refs_1_.4, bf16[128,1280]{1,0:T(8,128)(2,1)} %collective-permute-done.refs_2_, ...), custom_call_target="tpu_custom_call" | custom-call | tf_op jit(solution)/shard_map/shared_ab/pallas_call | solution.py:55
  19.2 4.8 %collective-permute-start.7 = (bf16[256,768]{1,0:T(8,128)(2,1)}, bf16[256,768]{1,0:T(8,128)(2,1)}, u32[]{:S(2)}, u32[]{:S(2)}) collective-permute-start(bf16[256,768]{1,0:T(8,128)(2,1)} %get-tuple-element.52), channel_id=1, source_target_pairs={{0,2},{1,3},{2,0},{3,1},{4,6},{5,7},{6,4},{7,5},{8,10},{9,11},{10,... | collective-permute-start | bytes 1179656 | tf_op jit(solution)/shard_map/ppermute | solution.py:450
  24.0 3.6 %shared_e.1 = (bf16[256,640]{1,0:T(8,128)(2,1)}, bf16[256,640]{1,0:T(8,128)(2,1)}, f32[128,768]{1,0:T(8,128)}, bf16[128,768]{1,0:T(8,128)(2,1)S(1)}) custom-call(s32[4]{0:T(128)S(1)} %pad_add_fusion.refs_0_.flag_ref, bf16[128,1280]{1,0:T(8,128)(2,1)} %refs_1_.5, bf16[128,1280]{1,0:T(8,128)(2,1)S(1)} %collective-permute-done.4.refs_2_, ...), custom_call_target="tpu_custom_call" | custom-call | tf_op jit(solution)/shard_map/shared_e/pallas_call | solution.py:55
  28.1 6.7 %all-to-all-start = ((bf16[16,8,2560]{2,1,0:T(8,128)(2,1)}), bf16[16,8,2560]{2,1,0:T(8,128)(2,1)}, u32[]{:S(2)}, u32[]{:S(2)}) async-start(bf16[16,8,2560]{2,1,0:T(8,128)(2,1)} %bitcast.12), calls=%async_computation | async-start | bytes 1310720 | tf_op jit(solution)/shard_map/all_to_all | solution.py:461
  36.6 10.7 %collective-permute-done.8.refs_3_ = bf16[128,768]{1,0:T(8,128)(2,1)S(1)} collective-permute-done((bf16[128,768]{1,0:T(8,128)(2,1)S(1)}, bf16[128,768]{1,0:T(8,128)(2,1)S(1)}, u32[]{:S(2)}, u32[]{:S(2)}) %collective-permute-start.8) | collective-permute-done | bytes 196640 | tf_op jit(solution)/shard_map/ppermute | solution.py:450
  47.4 2.3 %shared_slopes.1 = (bf16[384,384]{1,0:T(8,128)(2,1)S(1)}, bf16[384,384]{1,0:T(8,128)(2,1)}) custom-call(f32[256,768]{1,0:T(8,128)} %get-tuple-element.49.refs_6_.refs_0_, bf16[256,768]{1,0:T(8,128)(2,1)} %collective-permute-done.7.refs_1_, f32[128,768]{1,0:T(8,128)} %get-tuple-element.53.refs_2_, bf16[128,768]{1,0:T(8,128)(2,1)S(1)} %collective-permute-done.8.refs_3_, ...), custom_call_target="tpu_custom_call" | custom-call | tf_op jit(solution)/shard_map/shared_slopes/pallas_call | solution.py:55
  50.7 7.5 %collective-permute-done.9.refs_0_.refs_5_.refs_2_ = bf16[384,384]{1,0:T(8,128)(2,1)S(1)} collective-permute-done((bf16[384,384]{1,0:T(8,128)(2,1)S(1)}, bf16[384,384]{1,0:T(8,128)(2,1)S(1)}, u32[]{:S(2)}, u32[]{:S(2)}) %collective-permute-start.9) | collective-permute-done | bytes 294944 | tf_op jit(solution)/shard_map/ppermute | solution.py:422
  59.8 2.6 %shared_weight_grads.3 = (bf16[384,640]{1,0:T(8,128)(2,1)}, bf16[384,640]{1,0:T(8,128)(2,1)S(1)}, bf16[384,640]{1,0:T(8,128)(2,1)S(1)}) custom-call(bf16[256,640]{1,0:T(8,128)(2,1)} %get-tuple-element.47.refs_0_, bf16[256,640]{1,0:T(8,128)(2,1)} %collective-permute-done.3.refs_4_.refs_1_, bf16[256,640]{1,0:T(8,128)(2,1)} %get-tuple-element.50.refs_2_, ...), custom_call_target="tpu_custom_call" | custom-call | tf_op jit(solution)/shard_map/shared_weight_grads/pallas_call | solution.py:55
  64.0 4.1 %collective-permute-start.15 = (bf16[384,640]{1,0:T(8,128)(2,1)}, bf16[384,640]{1,0:T(8,128)(2,1)}, u32[]{:S(2)}, u32[]{:S(2)}) collective-permute-start(bf16[384,640]{1,0:T(8,128)(2,1)} %get-tuple-element.58.refs_0_), channel_id=1, source_target_pairs={{0,8},{24,16},{1,9},{25,17},{2,10},{26,18},{3,11},{27,19},{4,12},{... | collective-permute-start | bytes 1474568 | tf_op jit(solution)/shard_map/ppermute | solution.py:312
  70.1 2.8 %collective-permute-start.17 = (bf16[384,640]{1,0:T(8,128)(2,1)}, bf16[384,640]{1,0:T(8,128)(2,1)S(1)}, u32[]{:S(2)}, u32[]{:S(2)}) collective-permute-start(bf16[384,640]{1,0:T(8,128)(2,1)} %copy-done.10), channel_id=1, source_target_pairs={{0,8},{24,16},{1,9},{25,17},{2,10},{26,18},{3,11},{27,19},{4,12},{... | collective-permute-start | bytes 1474568 | tf_op jit(solution)/shard_map/ppermute | solution.py:312
  76.3 2.6 %shared_weight_grads.2 = (bf16[384,640]{1,0:T(8,128)(2,1)S(1)}, bf16[384,640]{1,0:T(8,128)(2,1)S(1)}, bf16[384,640]{1,0:T(8,128)(2,1)S(1)}) custom-call(bf16[256,640]{1,0:T(8,128)(2,1)} %get-tuple-element.47.refs_0_, bf16[256,640]{1,0:T(8,128)(2,1)} %collective-permute-done.3.refs_4_.refs_1_, bf16[256,640]{1,0:T(8,128)(2,1)} %get-tuple-element.50.refs_2_, ...), custom_call_target="tpu_custom_call" | custom-call | tf_op jit(solution)/shard_map/shared_weight_grads/pallas_call | solution.py:55
  81.1 7.3 %collective-permute-start.21 = (bf16[384,640]{1,0:T(8,128)(2,1)S(1)}, bf16[384,640]{1,0:T(8,128)(2,1)S(1)}, u32[]{:S(2)}, u32[]{:S(2)}) collective-permute-start(bf16[384,640]{1,0:T(8,128)(2,1)S(1)} %get-tuple-element.66.refs_0_), channel_id=1, source_target_pairs={{0,8},{24,16},{1,9},{25,17},{2,10},{26,18},{3,11},{27,19},{4,12},{... | collective-permute-start | bytes 1474568 | tf_op jit(solution)/shard_map/ppermute | solution.py:326
  88.4 10.5 %routed_expert.1 = (bf16[1,384,2560]{2,1,0:T(8,128)(2,1)}, bf16[1,384,2560]{2,1,0:T(8,128)(2,1)}, bf16[1,384,2560]{2,1,0:T(8,128)(2,1)}, bf16[128,1280]{1,0:T(8,128)(2,1)S(1)}, bf16[128,1280]{1,0:T(8,128)(2,1)S(1)}) custom-call(s32[4]{0:T(128)S(1)} %pad_add_fusion.refs_0_.flag_ref, bf16[128,2560]{1,0:T(8,128)(2,1)} %bitcast.8.x_ref, ...), custom_call_target="tpu_custom_call" | custom-call | tf_op jit(solution)/shard_map/routed_expert/pallas_call | solution.py:523
  103.4 4.3 %shared_dx.1 = (bf16[128,1280]{1,0:T(8,128)(2,1)S(1)}, bf16[128,1280]{1,0:T(8,128)(2,1)}, bf16[128,1280]{1,0:T(8,128)(2,1)}) custom-call(s32[4]{0:T(128)S(1)} %pad_add_fusion.refs_0_.flag_ref, bf16[384,384]{1,0:T(8,128)(2,1)S(1)} %copy-done.9, bf16[384,384]{1,0:T(8,128)(2,1)S(1)} %copy-done.3, bf16[384,384]{1,0:T(8,128)(2,1)} %hold.1.refs_4_.refs_3_, ...), custom_call_target="tpu_custom_call" | custom-call | tf_op jit(solution)/shard_map/shared_dx/pallas_call | solution.py:55
  109.3 4.4 %collective-permute-start.23 = (bf16[384,640]{1,0:T(8,128)(2,1)S(1)}, bf16[384,640]{1,0:T(8,128)(2,1)S(1)}, u32[]{:S(2)}, u32[]{:S(2)}) collective-permute-start(bf16[384,640]{1,0:T(8,128)(2,1)S(1)} %get-tuple-element.72), channel_id=1, source_target_pairs={{0,8},{24,16},{8,0},{16,24},{1,9},{25,17},{9,1},{17,25},{2,10},{26... | collective-permute-start | bytes 1474568 | tf_op jit(solution)/shard_map/ppermute | solution.py:337
  119.0 6.5 %collective-permute-start.29 = (bf16[384,640]{1,0:T(8,128)(2,1)S(1)}, bf16[384,640]{1,0:T(8,128)(2,1)S(1)}, u32[]{:S(2)}, u32[]{:S(2)}) collective-permute-start(bf16[384,640]{1,0:T(8,128)(2,1)S(1)} %get-tuple-element.79), channel_id=1, source_target_pairs={{0,8},{24,16},{8,0},{16,24},{1,9},{25,17},{9,1},{17,25},{2,10},{26... | collective-permute-start | bytes 1474568 | tf_op jit(solution)/shard_map/ppermute | solution.py:337
  130.2 9.1 %all-to-all-start.1 = ((bf16[16,8,1280]{2,1,0:T(8,128)(2,1)}), bf16[16,8,1280]{2,1,0:T(8,128)(2,1)}, u32[]{:S(2)}, u32[]{:S(2)}) async-start(bf16[16,8,1280]{2,1,0:T(8,128)(2,1)} %bitcast.9), calls=%async_computation.1 | async-start | bytes 655360 | tf_op jit(solution)/shard_map/all_to_all | solution.py:566
  144.5 4.5 %collective-permute-done.32.refs_4_ = bf16[384,640]{1,0:T(8,128)(2,1)S(1)} collective-permute-done((bf16[384,640]{1,0:T(8,128)(2,1)}, bf16[384,640]{1,0:T(8,128)(2,1)S(1)}, u32[]{:S(2)}, u32[]{:S(2)}) %collective-permute-start.32) | collective-permute-done | bytes 491552 | tf_op jit(solution)/shard_map/ppermute | solution.py:342
  150.6 2.5 %combine.1 = (bf16[128,1280]{1,0:T(8,128)(2,1)}, f32[6,128]{1,0:T(8,128)}) custom-call(s32[4]{0:T(128)S(1)} %pad_add_fusion.refs_0_.flag_ref, s32[6,128]{1,0:T(8,128)} %bitcast.14, s32[6,128]{1,0:T(8,128)} %bitcast.16, bf16[6,128]{1,0:T(8,128)(2,1)} %bitcast.18, bf16[128,1280]{1,0:T(8,128)(2,1)} %bitcast.10.refs_4_, ...), custom_call_target="tpu_custom_call" | custom-call | tf_op jit(solution)/shard_map/combine/pallas_call | solution.py:55
  155.6 5.3 %collective-permute-done.30 = bf16[384,640]{1,0:T(8,128)(2,1)} collective-permute-done((bf16[384,640]{1,0:T(8,128)(2,1)S(1)}, bf16[384,640]{1,0:T(8,128)(2,1)}, u32[]{:S(2)}, u32[]{:S(2)}) %collective-permute-start.30) | collective-permute-done | bytes 491552 | tf_op jit(solution)/shard_map/ppermute | solution.py:342
  163.0 11.0 %collective-permute-done.33 = bf16[384,640]{1,0:T(8,128)(2,1)S(1)} collective-permute-done((bf16[384,640]{1,0:T(8,128)(2,1)S(1)}, bf16[384,640]{1,0:T(8,128)(2,1)S(1)}, u32[]{:S(2)}, u32[]{:S(2)}) %collective-permute-start.33) | collective-permute-done | bytes 491552 | tf_op jit(solution)/shard_map/ppermute | solution.py:342
  (120 shorter events, 49.7 us)
Async XLA Ops:
  7.1 16.9 %collective-permute-start.4 = (bf16[128,1280]{1,0:T(8,128)(2,1)}, bf16[128,1280]{1,0:T(8,128)(2,1)S(1)}, u32[]{:S(2)}, u32[]{:S(2)}) collective-permute-start(bf16[128,1280]{1,0:T(8,128)(2,1)} %refs_1_.5), channel_id=1, source_target_pairs={{0,4},{2,0},{1,5},{3,1},{6,2},{4,6},{7,3},{5,7},{8,12},{10,8},{9,1... | collective-permute-start | bytes 983048 | tf_op jit(solution)/shard_map/ppermute | solution.py:408
  9.2 14.8 %collective-permute-start.5 = (bf16[128,1280]{1,0:T(8,128)(2,1)}, bf16[128,1280]{1,0:T(8,128)(2,1)}, u32[]{:S(2)}, u32[]{:S(2)}) collective-permute-start(bf16[128,1280]{1,0:T(8,128)(2,1)} %refs_1_.5), channel_id=1, source_target_pairs={{2,4},{3,5},{4,2},{5,3},{10,12},{11,13},{12,10},{13,11},{18,20},{1... | collective-permute-start | bytes 983048 | tf_op jit(solution)/shard_map/ppermute | solution.py:409
  19.2 28.1 %collective-permute-start.7 = (bf16[256,768]{1,0:T(8,128)(2,1)}, bf16[256,768]{1,0:T(8,128)(2,1)}, u32[]{:S(2)}, u32[]{:S(2)}) collective-permute-start(bf16[256,768]{1,0:T(8,128)(2,1)} %get-tuple-element.52), channel_id=1, source_target_pairs={{0,2},{1,3},{2,0},{3,1},{4,6},{5,7},{6,4},{7,5},{8,10},{9,11},{10,... | collective-permute-start | bytes 1179656 | tf_op jit(solution)/shard_map/ppermute | solution.py:450
  27.6 19.8 %collective-permute-start.6 = (bf16[256,640]{1,0:T(8,128)(2,1)}, bf16[256,640]{1,0:T(8,128)(2,1)S(1)}, u32[]{:S(2)}, u32[]{:S(2)}) collective-permute-start(bf16[256,640]{1,0:T(8,128)(2,1)} %get-tuple-element.51), channel_id=1, source_target_pairs={{0,1},{1,0},{2,3},{3,2},{4,5},{5,4},{6,7},{7,6},{8,9},{9,8},{10,11... | collective-permute-start | bytes 983048 | tf_op jit(solution)/shard_map/ppermute | solution.py:404
  27.6 19.8 %collective-permute-start.3 = (bf16[256,640]{1,0:T(8,128)(2,1)}, bf16[256,640]{1,0:T(8,128)(2,1)}, u32[]{:S(2)}, u32[]{:S(2)}) collective-permute-start(bf16[256,640]{1,0:T(8,128)(2,1)} %get-tuple-element.48), channel_id=1, source_target_pairs={{0,1},{1,0},{2,3},{3,2},{4,5},{5,4},{6,7},{7,6},{8,9},{9,8},{10,11... | collective-permute-start | bytes 983048 | tf_op jit(solution)/shard_map/ppermute | solution.py:404
  28.1 40.5 %all-to-all-start = ((bf16[16,8,2560]{2,1,0:T(8,128)(2,1)}), bf16[16,8,2560]{2,1,0:T(8,128)(2,1)}, u32[]{:S(2)}, u32[]{:S(2)}) async-start(bf16[16,8,2560]{2,1,0:T(8,128)(2,1)} %bitcast.12), calls=%async_computation | async-start | bytes 1310720 | tf_op jit(solution)/shard_map/all_to_all | solution.py:461
  64.0 15.2 %collective-permute-start.15 = (bf16[384,640]{1,0:T(8,128)(2,1)}, bf16[384,640]{1,0:T(8,128)(2,1)}, u32[]{:S(2)}, u32[]{:S(2)}) collective-permute-start(bf16[384,640]{1,0:T(8,128)(2,1)} %get-tuple-element.58.refs_0_), channel_id=1, source_target_pairs={{0,8},{24,16},{1,9},{25,17},{2,10},{26,18},{3,11},{27,19},{4,12},{... | collective-permute-start | bytes 1474568 | tf_op jit(solution)/shard_map/ppermute | solution.py:312
  68.6 19.9 %collective-permute-start.18 = (bf16[128,2560]{1,0:T(8,128)(2,1)}, bf16[128,2560]{1,0:T(8,128)(2,1)S(1)}, u32[]{:S(2)}, u32[]{:S(2)}) collective-permute-start(bf16[128,2560]{1,0:T(8,128)(2,1)} %bitcast.8.x_ref), channel_id=1, source_target_pairs={{0,4},{4,0},{1,5},{5,1},{2,6},{6,2},{3,7},{7,3},{8,12},{12,8},{9,1... | collective-permute-start | bytes 1966088 | tf_op jit(solution)/shard_map/ppermute | solution.py:483
  70.1 28.8 %collective-permute-start.17 = (bf16[384,640]{1,0:T(8,128)(2,1)}, bf16[384,640]{1,0:T(8,128)(2,1)S(1)}, u32[]{:S(2)}, u32[]{:S(2)}) collective-permute-start(bf16[384,640]{1,0:T(8,128)(2,1)} %copy-done.10), channel_id=1, source_target_pairs={{0,8},{24,16},{1,9},{25,17},{2,10},{26,18},{3,11},{27,19},{4,12},{... | collective-permute-start | bytes 1474568 | tf_op jit(solution)/shard_map/ppermute | solution.py:312
  80.4 19.5 %collective-permute-start.16 = (bf16[384,640]{1,0:T(8,128)(2,1)S(1)}, bf16[384,640]{1,0:T(8,128)(2,1)S(1)}, u32[]{:S(2)}, u32[]{:S(2)}) collective-permute-start(bf16[384,640]{1,0:T(8,128)(2,1)S(1)} %get-tuple-element.61.refs_1_.refs_2_), channel_id=1, source_target_pairs={{8,16},{16,8},{9,17},{17,9},{10,18},{18,10},{11,19},{19,11},{12,20... | collective-permute-start | bytes 1474568 | tf_op jit(solution)/shard_map/ppermute | solution.py:328
  81.1 26.5 %collective-permute-start.21 = (bf16[384,640]{1,0:T(8,128)(2,1)S(1)}, bf16[384,640]{1,0:T(8,128)(2,1)S(1)}, u32[]{:S(2)}, u32[]{:S(2)}) collective-permute-start(bf16[384,640]{1,0:T(8,128)(2,1)S(1)} %get-tuple-element.66.refs_0_), channel_id=1, source_target_pairs={{0,8},{24,16},{1,9},{25,17},{2,10},{26,18},{3,11},{27,19},{4,12},{... | collective-permute-start | bytes 1474568 | tf_op jit(solution)/shard_map/ppermute | solution.py:326
  100.7 13.0 %collective-permute-start.19 = (bf16[384,640]{1,0:T(8,128)(2,1)S(1)}, bf16[384,640]{1,0:T(8,128)(2,1)S(1)}, u32[]{:S(2)}, u32[]{:S(2)}) collective-permute-start(bf16[384,640]{1,0:T(8,128)(2,1)S(1)} %get-tuple-element.64), channel_id=1, source_target_pairs={{0,8},{24,16},{8,0},{16,24},{1,9},{25,17},{9,1},{17,25},{2,10},{26... | collective-permute-start | bytes 1474568 | tf_op jit(solution)/shard_map/ppermute | solution.py:337
  101.8 12.9 %collective-permute-start.25 = (bf16[128,1280]{1,0:T(8,128)(2,1)S(1)}, bf16[128,1280]{1,0:T(8,128)(2,1)S(1)}, u32[]{:S(2)}, u32[]{:S(2)}) collective-permute-start(bf16[128,1280]{1,0:T(8,128)(2,1)S(1)} %get-tuple-element.74), channel_id=1, source_target_pairs={{0,4},{4,0},{1,5},{5,1},{2,6},{6,2},{3,7},{7,3},{8,12},{12,8},{9,1... | collective-permute-start | bytes 983048 | tf_op jit(solution)/shard_map/ppermute | solution.py:544
  109.3 16.3 %collective-permute-start.23 = (bf16[384,640]{1,0:T(8,128)(2,1)S(1)}, bf16[384,640]{1,0:T(8,128)(2,1)S(1)}, u32[]{:S(2)}, u32[]{:S(2)}) collective-permute-start(bf16[384,640]{1,0:T(8,128)(2,1)S(1)} %get-tuple-element.72), channel_id=1, source_target_pairs={{0,8},{24,16},{8,0},{16,24},{1,9},{25,17},{9,1},{17,25},{2,10},{26... | collective-permute-start | bytes 1474568 | tf_op jit(solution)/shard_map/ppermute | solution.py:337
  113.8 14.2 %collective-permute-start.22 = (bf16[384,640]{1,0:T(8,128)(2,1)S(1)}, bf16[384,640]{1,0:T(8,128)(2,1)S(1)}, u32[]{:S(2)}, u32[]{:S(2)}) collective-permute-start(bf16[384,640]{1,0:T(8,128)(2,1)S(1)} %line_sum.9.refs_4_.refs_0_), channel_id=1, source_target_pairs={{8,16},{16,8},{9,17},{17,9},{10,18},{18,10},{11,19},{19,11},{12,20... | collective-permute-start | bytes 1474568 | tf_op jit(solution)/shard_map/ppermute | solution.py:328
  115.5 33.5 %collective-permute-start.26 = (bf16[128,1280]{1,0:T(8,128)(2,1)}, bf16[128,1280]{1,0:T(8,128)(2,1)}, u32[]{:S(2)}, u32[]{:S(2)}) collective-permute-start(bf16[128,1280]{1,0:T(8,128)(2,1)} %get-tuple-element.76), channel_id=1, source_target_pairs={{4,0},{0,2},{5,1},{1,3},{2,6},{6,4},{3,7},{7,5},{12,8},{8,10},{13,... | collective-permute-start | bytes 983048 | tf_op jit(solution)/shard_map/ppermute | solution.py:578
  116.9 32.1 %collective-permute-start.27 = (bf16[128,1280]{1,0:T(8,128)(2,1)}, bf16[128,1280]{1,0:T(8,128)(2,1)}, u32[]{:S(2)}, u32[]{:S(2)}) collective-permute-start(bf16[128,1280]{1,0:T(8,128)(2,1)} %get-tuple-element.78), channel_id=1, source_target_pairs={{2,4},{3,5},{4,2},{5,3},{10,12},{11,13},{12,10},{13,11},{18,20},{1... | collective-permute-start | bytes 983048 | tf_op jit(solution)/shard_map/ppermute | solution.py:579
  119.0 21.2 %collective-permute-start.29 = (bf16[384,640]{1,0:T(8,128)(2,1)S(1)}, bf16[384,640]{1,0:T(8,128)(2,1)S(1)}, u32[]{:S(2)}, u32[]{:S(2)}) collective-permute-start(bf16[384,640]{1,0:T(8,128)(2,1)S(1)} %get-tuple-element.79), channel_id=1, source_target_pairs={{0,8},{24,16},{8,0},{16,24},{1,9},{25,17},{9,1},{17,25},{2,10},{26... | collective-permute-start | bytes 1474568 | tf_op jit(solution)/shard_map/ppermute | solution.py:337
  125.7 15.4 %collective-permute-start.28 = (bf16[384,640]{1,0:T(8,128)(2,1)S(1)}, bf16[384,640]{1,0:T(8,128)(2,1)}, u32[]{:S(2)}, u32[]{:S(2)}) collective-permute-start(bf16[384,640]{1,0:T(8,128)(2,1)S(1)} %line_sum.10.refs_2_.refs_0_), channel_id=1, source_target_pairs={{8,16},{16,8},{9,17},{17,9},{10,18},{18,10},{11,19},{19,11},{12,20... | collective-permute-start | bytes 1474568 | tf_op jit(solution)/shard_map/ppermute | solution.py:328
  129.0 20.0 %collective-permute-start.32 = (bf16[384,640]{1,0:T(8,128)(2,1)}, bf16[384,640]{1,0:T(8,128)(2,1)S(1)}, u32[]{:S(2)}, u32[]{:S(2)}) collective-permute-start(bf16[384,640]{1,0:T(8,128)(2,1)} %get-tuple-element.80.refs_2_), channel_id=1, source_target_pairs={{8,0},{16,24},{9,1},{17,25},{10,2},{18,26},{11,3},{19,27},{12,4},{... | collective-permute-start | bytes 1474568 | tf_op jit(solution)/shard_map/ppermute | solution.py:342
  130.2 20.3 %all-to-all-start.1 = ((bf16[16,8,1280]{2,1,0:T(8,128)(2,1)}), bf16[16,8,1280]{2,1,0:T(8,128)(2,1)}, u32[]{:S(2)}, u32[]{:S(2)}) async-start(bf16[16,8,1280]{2,1,0:T(8,128)(2,1)} %bitcast.9), calls=%async_computation.1 | async-start | bytes 655360 | tf_op jit(solution)/shard_map/all_to_all | solution.py:566
  140.3 12.7 %collective-permute-start.31 = (bf16[384,640]{1,0:T(8,128)(2,1)S(1)}, bf16[384,640]{1,0:T(8,128)(2,1)S(1)}, u32[]{:S(2)}, u32[]{:S(2)}) collective-permute-start(bf16[384,640]{1,0:T(8,128)(2,1)S(1)} %line_sum.11.refs_2_.refs_0_), channel_id=1, source_target_pairs={{8,16},{16,8},{9,17},{17,9},{10,18},{18,10},{11,19},{19,11},{12,20... | collective-permute-start | bytes 1474568 | tf_op jit(solution)/shard_map/ppermute | solution.py:328
  142.3 18.6 %collective-permute-start.30 = (bf16[384,640]{1,0:T(8,128)(2,1)S(1)}, bf16[384,640]{1,0:T(8,128)(2,1)}, u32[]{:S(2)}, u32[]{:S(2)}) collective-permute-start(bf16[384,640]{1,0:T(8,128)(2,1)S(1)} %line_total.10.refs_8_.refs_2_), channel_id=1, source_target_pairs={{8,0},{16,24},{9,1},{17,25},{10,2},{18,26},{11,3},{19,27},{12,4},{... | collective-permute-start | bytes 1474568 | tf_op jit(solution)/shard_map/ppermute | solution.py:342
  153.2 20.9 %collective-permute-start.33 = (bf16[384,640]{1,0:T(8,128)(2,1)S(1)}, bf16[384,640]{1,0:T(8,128)(2,1)S(1)}, u32[]{:S(2)}, u32[]{:S(2)}) collective-permute-start(bf16[384,640]{1,0:T(8,128)(2,1)S(1)} %line_total.11), channel_id=1, source_target_pairs={{8,0},{16,24},{9,1},{17,25},{10,2},{18,26},{11,3},{19,27},{12,4},{... | collective-permute-start | bytes 1474568 | tf_op jit(solution)/shard_map/ppermute | solution.py:342
  (31 other events, 221.9 us)
